TPU v7x, 1024 devices: a whole 4x4x32 slice. The times are simulated.
1024 devices in a mesh: ty: 32 (over x, z_hi, y), tx: 16 (over z_lo), corner: 2 (over core).
Axes of the slice: x: 4, y: 4, z: 32 (z_hi: 2, z_lo: 16; z = z_hi * 16 + z_lo), core: 2. Of those that a mesh axis runs over, the one named last changes fastest.
Arguments:
- level_init: int32 [8192, 4096], P('ty', 'tx'), may hold values from -64 to 64
- target: int32 [8192, 4096], P('ty', 'tx'), may hold values 0 or 1
- kernels: float32 [2, 5, 2, 128, 128], P('corner'), may hold values from -12 to 12
- corner_doses: float32 [2], P('corner'), may hold values from 0.7 to 1.4
Outputs:
- resist: float32 [2, 8192, 4096], P('corner', 'ty', 'tx')
- level_set: float32 [8192, 4096], P('ty', 'tx')
All inputs are finite; a program needn't handle non-finite values. No bound on the sum of `target` on one device may be relied on, other than what follows from the above.
Results may differ from a plain program's by a relative error of at most 0.015.
The roundings to bfloat16 on the way count: a program that leaves them out, or rounds other values in their place, can miss the bound.
Values may be sent and summed in bfloat16 or wider, within the bound.
A program may use at most 32 MiB of HBM per device.

v0:
```python
import math

import jax
import jax.numpy as jnp
from jax import lax
from jax.sharding import PartitionSpec as P

HALO = 128
KF = 128
LS_STEPS = 3


STEEPNESS = 4.0
THRESHOLD = 1.0
SPEED_GAIN = 4.0
SMOOTHING = 0.24
GRAD_FLOOR = 0.25


def with_halo(block, sides, width):
    for axis, dim in sides:
        count = lax.axis_size(axis)
        forward = [(i, i + 1) for i in range(count - 1)]
        backward = [(target, source) for source, target in forward]
        low = lax.ppermute(
            lax.slice_in_dim(block, block.shape[dim] - width, None, axis=dim), axis, forward
        )
        high = lax.ppermute(lax.slice_in_dim(block, 0, width, axis=dim), axis, backward)
        block = jnp.concatenate([low, block, high], axis=dim)
    return block


def make_tables(window, freqs, margin, tile):
    shifts = jnp.arange(freqs, dtype=jnp.int32) - freqs // 2
    places = jnp.arange(window, dtype=jnp.int32)
    phases = shifts[:, None] * places[None, :] % window
    angles = 2.0 * math.pi / window * phases.astype(jnp.float32)
    scaled = 1.0 / math.sqrt(window)
    fwd_cos = (jnp.cos(angles) * scaled).astype(jnp.bfloat16)
    fwd_sin = (-jnp.sin(angles) * scaled).astype(jnp.bfloat16)
    inner = angles[:, margin : margin + tile].T
    inv_cos = (jnp.cos(inner) * scaled).astype(jnp.bfloat16)
    inv_sin = (jnp.sin(inner) * scaled).astype(jnp.bfloat16)
    return (fwd_cos, fwd_sin, inv_cos, inv_sin)


def matmul(left, right):
    return jnp.dot(left, right, preferred_element_type=jnp.float32)


def batched(form, left, right):
    return jnp.einsum(form, left, right, preferred_element_type=jnp.float32)


def tile_pass(win_data, goal, kernel_re, kernel_im, doses_col, tables):
    fwd_cos, fwd_sin, inv_cos, inv_sin = tables
    freqs = fwd_cos.shape[0]
    lift = matmul(jnp.concatenate([fwd_cos, fwd_sin], axis=0), win_data).astype(jnp.bfloat16)
    lift_re = lift[:freqs]
    lift_im = lift[freqs:]
    spec_re = matmul(lift_re, fwd_cos.T) - matmul(lift_im, fwd_sin.T)
    spec_im = matmul(lift_re, fwd_sin.T) + matmul(lift_im, fwd_cos.T)
    blur_re = (kernel_re * spec_re - kernel_im * spec_im).astype(jnp.bfloat16)
    blur_im = (kernel_re * spec_im + kernel_im * spec_re).astype(jnp.bfloat16)
    proj_re = (
        batched("rj,gjk->grk", inv_cos, blur_re) - batched("rj,gjk->grk", inv_sin, blur_im)
    ).astype(jnp.bfloat16)
    proj_im = (
        batched("rj,gjk->grk", inv_cos, blur_im) + batched("rj,gjk->grk", inv_sin, blur_re)
    ).astype(jnp.bfloat16)
    field_re = batched("grj,cj->grc", proj_re, inv_cos) - batched("grj,cj->grc", proj_im, inv_sin)
    field_im = batched("grj,cj->grc", proj_re, inv_sin) + batched("grj,cj->grc", proj_im, inv_cos)
    groups = doses_col.shape[0]
    tile = field_re.shape[1]
    grouped = (groups, -1, tile, tile)
    power = (field_re * field_re + field_im * field_im).reshape(grouped)
    intensity = jnp.sum(power, axis=1)
    dose_col = doses_col[:, None, None]
    resist = jax.nn.sigmoid(STEEPNESS * (dose_col * intensity - THRESHOLD))
    sens = 2.0 * (resist - goal) * STEEPNESS * dose_col * resist * (1.0 - resist)
    adj_re = (
        (2.0 * sens[:, None] * field_re.reshape(grouped))
        .reshape(field_re.shape)
        .astype(jnp.bfloat16)
    )
    adj_im = (
        (2.0 * sens[:, None] * field_im.reshape(grouped))
        .reshape(field_im.shape)
        .astype(jnp.bfloat16)
    )
    back_re = (
        batched("grc,cj->grj", adj_re, inv_cos) + batched("grc,cj->grj", adj_im, inv_sin)
    ).astype(jnp.bfloat16)
    back_im = (
        batched("grc,cj->grj", adj_im, inv_cos) - batched("grc,cj->grj", adj_re, inv_sin)
    ).astype(jnp.bfloat16)
    grad_blur_re = batched("rj,grk->gjk", inv_cos, back_re) + batched(
        "rj,grk->gjk", inv_sin, back_im
    )
    grad_blur_im = batched("rj,grk->gjk", inv_cos, back_im) - batched(
        "rj,grk->gjk", inv_sin, back_re
    )
    grad_spec_re = jnp.sum(kernel_re * grad_blur_re + kernel_im * grad_blur_im, axis=0)
    grad_spec_im = jnp.sum(kernel_re * grad_blur_im - kernel_im * grad_blur_re, axis=0)
    return (resist, grad_spec_re, grad_spec_im)


def window_grad(grad_spec_re, grad_spec_im, tables):
    fwd_cos, fwd_sin = (tables[0], tables[1])
    spec_low_re = grad_spec_re.astype(jnp.bfloat16)
    spec_low_im = grad_spec_im.astype(jnp.bfloat16)
    grad_lift_re = (matmul(spec_low_re, fwd_cos) + matmul(spec_low_im, fwd_sin)).astype(
        jnp.bfloat16
    )
    grad_lift_im = (matmul(spec_low_im, fwd_cos) - matmul(spec_low_re, fwd_sin)).astype(
        jnp.bfloat16
    )
    stacked = jnp.concatenate([fwd_cos, fwd_sin], axis=0)
    grad_lift = jnp.concatenate([grad_lift_re, grad_lift_im], axis=0)
    result = lax.dot_general(
        stacked, grad_lift, (((0,), (0,)), ((), ())), preferred_element_type=jnp.float32
    )
    return result.astype(jnp.bfloat16)


def fold_axis(values, tile, margin, axis):
    centre = lax.slice_in_dim(values, 2 * margin, 2 * margin + tile, axis=axis)
    upper_rim = lax.slice_in_dim(values, 0, margin, axis=axis)
    lower_rim = lax.slice_in_dim(values, tile + 3 * margin, tile + 4 * margin, axis=axis)
    leading = [(0, 0), (0, 0)]
    trailing = [(0, 0), (0, 0)]
    leading[axis] = (0, tile - margin)
    trailing[axis] = (tile - margin, 0)
    return centre + jnp.pad(upper_rim, leading) + jnp.pad(lower_rim, trailing)


def advance(padded, speed):
    centre = padded[1:-1, 1:-1]
    above_cells = padded[:-2, 1:-1]
    below_cells = padded[2:, 1:-1]
    left_cells = padded[1:-1, :-2]
    right_cells = padded[1:-1, 2:]
    slope_y = 0.5 * (below_cells - above_cells)
    slope_x = 0.5 * (right_cells - left_cells)
    spread = above_cells + below_cells + left_cells + right_cells - 4.0 * centre
    return (
        centre
        - SPEED_GAIN * speed * jnp.sqrt(GRAD_FLOOR + slope_y * slope_y + slope_x * slope_x)
        + SMOOTHING * spread
    )


def body(level_init, target, kernels, corner_doses):
    tile = level_init.shape[0]
    margin = HALO
    freqs = KF
    window = tile + 2 * margin
    tables = make_tables(window, freqs, margin, tile)
    level = level_init.astype(jnp.float32) * 0.125
    trans = jnp.tanh(0.25 * level)
    level_rim = with_halo(level.astype(jnp.bfloat16), (("ty", 0), ("tx", 1)), margin).astype(
        level.dtype
    )
    win_data = jnp.tanh(0.25 * level_rim).astype(jnp.bfloat16)
    kernel_re = kernels[:, :, 0].reshape(-1, freqs, freqs)
    kernel_im = kernels[:, :, 1].reshape(-1, freqs, freqs)
    resist, grad_spec_re, grad_spec_im = tile_pass(
        win_data, target.astype(jnp.float32), kernel_re, kernel_im, corner_doses, tables
    )
    grad_spec_re, grad_spec_im = (
        lax.psum(grad_spec_re.astype(jnp.bfloat16), "corner").astype(jnp.float32),
        lax.psum(grad_spec_im.astype(jnp.bfloat16), "corner").astype(jnp.float32),
    )
    grad_window = window_grad(grad_spec_re, grad_spec_im, tables)
    framed_grad = with_halo(grad_window, (("ty", 0), ("tx", 1)), margin).astype(jnp.float32)
    grad_trans = fold_axis(fold_axis(framed_grad, tile, margin, 0), tile, margin, 1)
    speed = grad_trans * 0.25 * (1.0 - trans * trans)
    for repeat in range(LS_STEPS):
        padded = with_halo(level.astype(jnp.bfloat16), (("ty", 0), ("tx", 1)), 1).astype(
            level.dtype
        )
        level = advance(padded, speed)
    return (resist, level)


def solution(mesh):
    in_specs = (P("ty", "tx"), P("ty", "tx"), P("corner", None, None, None, None), P("corner"))
    out_specs = (P("corner", "ty", "tx"), P("ty", "tx"))
    return jax.shard_map(body, mesh=mesh, in_specs=in_specs, out_specs=out_specs, check_vma=False)
```

profile of v0, /device:TPU:24, one launch (start us, length us, event | category | flops | bytes accessed | tf_op | source)
XLA Modules:
  0.0 319.0 jit_solution(9726610921038797144)
XLA Ops:
  7.2 1.0 multiply_convert_fusion.2
  8.2 28.6 %collective-permute-start = (bf16[128,256]{1,0:T(8,128)(2,1)S(1)}, bf16[128,256]{1,0:T(8,128)(2,1)S(1)}, u32[]{:S(2)}, u32[]{:S(2)}) collective-permute-start(bf16[128,256]{1,0:T(8,128)(2,1)S(1)} %get-tuple-element.34), channel_id=1, source_target_pairs={{0,32},{32,64},{64,96},{96,128},{128,160},{160,192},{192,224},{224... | collective-permute-start | bytes 196616 | tf_op jit(solution)/shard_map/ppermute | solution.py:25
  36.8 1.9 collective-permute-start.1
  38.8 1.1 fusion.101
  39.9 1.1 fusion.32
  42.1 21.6 %collective-permute-done.1 = bf16[128,256]{1,0:T(8,128)(2,1)S(1)} collective-permute-done((bf16[128,256]{1,0:T(8,128)(2,1)S(1)}, bf16[128,256]{1,0:T(8,128)(2,1)S(1)}, u32[]{:S(2)}, u32[]{:S(2)}) %collective-permute-start.1) | collective-permute-done | bytes 65568 | tf_op jit(solution)/shard_map/ppermute | solution.py:28
  63.7 12.5 %collective-permute-start.2 = (bf16[512,128]{1,0:T(8,128)(2,1)S(1)}, bf16[512,128]{1,0:T(8,128)(2,1)S(1)}, u32[]{:S(2)}, u32[]{:S(2)}) collective-permute-start(bf16[512,128]{1,0:T(8,128)(2,1)S(1)} %get-tuple-element.20), channel_id=1, source_target_pairs={{0,2},{2,4},{4,6},{6,8},{8,10},{10,12},{12,14},{14,16},{16,18},{18... | collective-permute-start | bytes 393224 | tf_op jit(solution)/shard_map/ppermute | solution.py:25
  76.2 1.3 collective-permute-start.3
  77.5 0.5 fusion.55
  78.0 0.7 collective-permute-done.2
  78.7 4.4 %collective-permute-done.3 = bf16[512,128]{1,0:T(8,128)(2,1)S(1)} collective-permute-done((bf16[512,128]{1,0:T(8,128)(2,1)S(1)}, bf16[512,128]{1,0:T(8,128)(2,1)S(1)}, u32[]{:S(2)}, u32[]{:S(2)}) %collective-permute-start.3) | collective-permute-done | bytes 131104 | tf_op jit(solution)/shard_map/ppermute | solution.py:28
  83.1 0.3 convolution_convert_fusion.1
  83.5 1.2 fusion.47
  84.7 1.2 fusion.46
  85.9 1.2 convolution_add_fusion.5
  87.2 1.2 convolution_subtract_fusion.5
  89.3 0.4 fusion.114
  89.6 0.4 fusion.112
  90.2 0.4 convolution_subtract_fusion
  90.6 0.4 add_reduce_fusion
  91.0 0.5 copy-done.1
  91.6 0.8 multiply_multiply_fusion
  92.4 0.3 fusion.48
  92.7 0.3 fusion.49
  93.1 0.4 fusion.3
  93.4 0.3 fusion.2
  94.4 0.3 fusion.7
  94.7 1.0 fusion.27
  95.7 40.9 %all-reduce.5.cloned.1.call-done = (bf16[128,128]{0,1:T(8,128)(2,1)}, bf16[128,128]{0,1:T(8,128)(2,1)}) async-done(((bf16[128,128]{0,1:T(8,128)(2,1)}, bf16[128,128]{0,1:T(8,128)(2,1)}), (bf16[128,128]{0,1:T(8,128)(2,1)}, bf16[128,128]{0,1:T(8,128)(2,1)})) %all-reduce.5.cloned.1.call-update) | async-done | bytes 65552 | tf_op jit(solution)/shard_map/psum | solution.py:172
  136.6 2.0 fusion.44
  138.5 2.0 fusion.45
  140.5 1.4 fusion.9
  141.9 1.2 fusion.8
  143.1 0.3 convolution_convert_fusion
  143.5 23.1 %collective-permute-start.8 = (bf16[128,512]{1,0:T(8,128)(2,1)S(1)}, bf16[128,512]{1,0:T(8,128)(2,1)S(1)}, u32[]{:S(2)}, u32[]{:S(2)}) collective-permute-start(bf16[128,512]{1,0:T(8,128)(2,1)S(1)} %get-tuple-element.14), channel_id=1, source_target_pairs={{0,32},{32,64},{64,96},{96,128},{128,160},{160,192},{192,224},{224... | collective-permute-start | bytes 393224 | tf_op jit(solution)/shard_map/ppermute | solution.py:25
  166.6 1.9 collective-permute-start.9
  168.5 24.4 %collective-permute-start.4 = (bf16[1,256]{1,0:T(2,128)(2,1)S(1)}, bf16[1,256]{1,0:T(2,128)(2,1)S(1)}, u32[]{:S(2)}, u32[]{:S(2)}) collective-permute-start(bf16[1,256]{1,0:T(2,128)(2,1)S(1)} %get-tuple-element.32), channel_id=1, source_target_pairs={{0,32},{32,64},{64,96},{96,128},{128,160},{160,192},{192,224},{224... | collective-permute-start | bytes 1544 | tf_op jit(solution)/shard_map/ppermute | solution.py:25
  192.9 1.9 collective-permute-start.5
  194.8 24.0 %collective-permute-done.5 = bf16[1,256]{1,0:T(2,128)(2,1)S(1)} collective-permute-done((bf16[1,256]{1,0:T(2,128)(2,1)S(1)}, bf16[1,256]{1,0:T(2,128)(2,1)S(1)}, u32[]{:S(2)}, u32[]{:S(2)}) %collective-permute-start.5) | collective-permute-done | bytes 544 | tf_op jit(solution)/shard_map/ppermute | solution.py:28
  218.9 2.6 collective-permute-start.10
  221.5 1.3 collective-permute-start.11
  222.8 4.5 %collective-permute-start.6 = (bf16[258,1]{1,0:T(8,128)(2,1)S(1)}, bf16[258,1]{1,0:T(8,128)(2,1)S(1)}, u32[]{:S(2)}, u32[]{:S(2)}) collective-permute-start(bf16[258,1]{1,0:T(8,128)(2,1)S(1)} %get-tuple-element.26), channel_id=1, source_target_pairs={{0,2},{2,4},{4,6},{6,8},{8,10},{10,12},{12,14},{14,16},{16,18},{18... | collective-permute-start | bytes 1556 | tf_op jit(solution)/shard_map/ppermute | solution.py:25
  227.4 1.3 collective-permute-start.7
  228.7 0.6 collective-permute-done.6
  229.3 4.3 %collective-permute-done.7 = bf16[258,1]{1,0:T(8,128)(2,1)S(1)} collective-permute-done((bf16[258,1]{1,0:T(8,128)(2,1)S(1)}, bf16[258,1]{1,0:T(8,128)(2,1)S(1)}, u32[]{:S(2)}, u32[]{:S(2)}) %collective-permute-start.7) | collective-permute-done | bytes 548 | tf_op jit(solution)/shard_map/ppermute | solution.py:28
  234.0 0.5 copy-done.2
  234.6 0.8 copy-done
  235.4 0.4 add_convert_fusion.1
  235.9 1.9 collective-permute-start.12
  237.8 3.9 %collective-permute-start.13 = (bf16[1,256]{1,0:T(2,128)(2,1)S(1)}, bf16[1,256]{1,0:T(2,128)(2,1)S(1)}, u32[]{:S(2)}, u32[]{:S(2)}) collective-permute-start(bf16[1,256]{1,0:T(2,128)(2,1)S(1)} %get-tuple-element.31), channel_id=1, source_target_pairs={{32,0},{64,32},{96,64},{128,96},{160,128},{192,160},{224,192},{256... | collective-permute-start | bytes 1544 | tf_op jit(solution)/shard_map/ppermute | solution.py:28
  241.7 22.0 %collective-permute-done.13 = bf16[1,256]{1,0:T(2,128)(2,1)S(1)} collective-permute-done((bf16[1,256]{1,0:T(2,128)(2,1)S(1)}, bf16[1,256]{1,0:T(2,128)(2,1)S(1)}, u32[]{:S(2)}, u32[]{:S(2)}) %collective-permute-start.13) | collective-permute-done | bytes 544 | tf_op jit(solution)/shard_map/ppermute | solution.py:28
  263.8 2.6 collective-permute-start.14
  266.4 1.3 collective-permute-start.15
  267.7 0.6 collective-permute-done.14
  268.3 4.3 %collective-permute-done.15 = bf16[258,1]{1,0:T(8,128)(2,1)S(1)} collective-permute-done((bf16[258,1]{1,0:T(8,128)(2,1)S(1)}, bf16[258,1]{1,0:T(8,128)(2,1)S(1)}, u32[]{:S(2)}, u32[]{:S(2)}) %collective-permute-start.15) | collective-permute-done | bytes 548 | tf_op jit(solution)/shard_map/ppermute | solution.py:28
  272.8 0.4 add_convert_fusion
  273.2 1.9 collective-permute-start.16
  275.1 3.9 %collective-permute-start.17 = (bf16[1,256]{1,0:T(2,128)(2,1)S(1)}, bf16[1,256]{1,0:T(2,128)(2,1)S(1)}, u32[]{:S(2)}, u32[]{:S(2)}) collective-permute-start(bf16[1,256]{1,0:T(2,128)(2,1)S(1)} %get-tuple-element.29), channel_id=1, source_target_pairs={{32,0},{64,32},{96,64},{128,96},{160,128},{192,160},{224,192},{256... | collective-permute-start | bytes 1544 | tf_op jit(solution)/shard_map/ppermute | solution.py:28
  279.0 22.0 %collective-permute-done.17 = bf16[1,256]{1,0:T(2,128)(2,1)S(1)} collective-permute-done((bf16[1,256]{1,0:T(2,128)(2,1)S(1)}, bf16[1,256]{1,0:T(2,128)(2,1)S(1)}, u32[]{:S(2)}, u32[]{:S(2)}) %collective-permute-start.17) | collective-permute-done | bytes 544 | tf_op jit(solution)/shard_map/ppermute | solution.py:28
  301.1 3.6 %collective-permute-start.18 = (bf16[258,1]{1,0:T(8,128)(2,1)S(1)}, bf16[258,1]{1,0:T(8,128)(2,1)S(1)}, u32[]{:S(2)}, u32[]{:S(2)}) collective-permute-start(bf16[258,1]{1,0:T(8,128)(2,1)S(1)} %get-tuple-element.22), channel_id=1, source_target_pairs={{0,2},{2,4},{4,6},{6,8},{8,10},{10,12},{12,14},{14,16},{16,18},{18... | collective-permute-start | bytes 1556 | tf_op jit(solution)/shard_map/ppermute | solution.py:25
  304.8 1.3 collective-permute-start.19
  306.1 0.6 collective-permute-done.18
  306.7 4.3 %collective-permute-done.19 = bf16[258,1]{1,0:T(8,128)(2,1)S(1)} collective-permute-done((bf16[258,1]{1,0:T(8,128)(2,1)S(1)}, bf16[258,1]{1,0:T(8,128)(2,1)S(1)}, u32[]{:S(2)}, u32[]{:S(2)}) %collective-permute-start.19) | collective-permute-done | bytes 548 | tf_op jit(solution)/shard_map/ppermute | solution.py:28
  311.1 1.1 multiply_add_fusion
  (50 shorter events, 3.5 us)
Async XLA Ops:
  7.2 129.4 %all-reduce.5.cloned.1.call-start = ((), (), s32[]{:S(2)}) async-start(), calls=%async_computation | async-start | bytes 131072 | tf_op jit(solution)/shard_map/psum | solution.py:172
  8.2 33.8 %collective-permute-start = (bf16[128,256]{1,0:T(8,128)(2,1)S(1)}, bf16[128,256]{1,0:T(8,128)(2,1)S(1)}, u32[]{:S(2)}, u32[]{:S(2)}) collective-permute-start(bf16[128,256]{1,0:T(8,128)(2,1)S(1)} %get-tuple-element.34), channel_id=1, source_target_pairs={{0,32},{32,64},{64,96},{96,128},{128,160},{160,192},{192,224},{224... | collective-permute-start | bytes 196616 | tf_op jit(solution)/shard_map/ppermute | solution.py:25
  36.8 26.8 %collective-permute-start.1 = (bf16[128,256]{1,0:T(8,128)(2,1)S(1)}, bf16[128,256]{1,0:T(8,128)(2,1)S(1)}, u32[]{:S(2)}, u32[]{:S(2)}) collective-permute-start(bf16[128,256]{1,0:T(8,128)(2,1)S(1)} %get-tuple-element.35), channel_id=1, source_target_pairs={{32,0},{64,32},{96,64},{128,96},{160,128},{192,160},{224,192},{256... | collective-permute-start | bytes 196616 | tf_op jit(solution)/shard_map/ppermute | solution.py:28
  63.7 15.0 %collective-permute-start.2 = (bf16[512,128]{1,0:T(8,128)(2,1)S(1)}, bf16[512,128]{1,0:T(8,128)(2,1)S(1)}, u32[]{:S(2)}, u32[]{:S(2)}) collective-permute-start(bf16[512,128]{1,0:T(8,128)(2,1)S(1)} %get-tuple-element.20), channel_id=1, source_target_pairs={{0,2},{2,4},{4,6},{6,8},{8,10},{10,12},{12,14},{14,16},{16,18},{18... | collective-permute-start | bytes 393224 | tf_op jit(solution)/shard_map/ppermute | solution.py:25
  76.2 6.9 %collective-permute-start.3 = (bf16[512,128]{1,0:T(8,128)(2,1)S(1)}, bf16[512,128]{1,0:T(8,128)(2,1)S(1)}, u32[]{:S(2)}, u32[]{:S(2)}) collective-permute-start(bf16[512,128]{1,0:T(8,128)(2,1)S(1)} %get-tuple-element.21), channel_id=1, source_target_pairs={{2,0},{4,2},{6,4},{8,6},{10,8},{12,10},{14,12},{16,14},{18,16},{20... | collective-permute-start | bytes 393224 | tf_op jit(solution)/shard_map/ppermute | solution.py:28
  90.6 1.0 copy-start.1
  136.6 3.9 %copy-start.4 = (bf16[128,128]{0,1:T(8,128)(2,1)S(1)}, bf16[128,128]{0,1:T(8,128)(2,1)}, u32[]{:S(2)}) copy-start(bf16[128,128]{0,1:T(8,128)(2,1)} %get-tuple-element.5) | copy-start | bytes 98308
  138.5 3.4 %copy-start.3 = (bf16[128,128]{0,1:T(8,128)(2,1)S(1)}, bf16[128,128]{0,1:T(8,128)(2,1)}, u32[]{:S(2)}) copy-start(bf16[128,128]{0,1:T(8,128)(2,1)} %get-tuple-element.4) | copy-start | bytes 98308
  143.5 75.4 %collective-permute-start.8 = (bf16[128,512]{1,0:T(8,128)(2,1)S(1)}, bf16[128,512]{1,0:T(8,128)(2,1)S(1)}, u32[]{:S(2)}, u32[]{:S(2)}) collective-permute-start(bf16[128,512]{1,0:T(8,128)(2,1)S(1)} %get-tuple-element.14), channel_id=1, source_target_pairs={{0,32},{32,64},{64,96},{96,128},{128,160},{160,192},{192,224},{224... | collective-permute-start | bytes 393224 | tf_op jit(solution)/shard_map/ppermute | solution.py:25
  166.6 52.3 %collective-permute-start.9 = (bf16[128,512]{1,0:T(8,128)(2,1)S(1)}, bf16[128,512]{1,0:T(8,128)(2,1)S(1)}, u32[]{:S(2)}, u32[]{:S(2)}) collective-permute-start(bf16[128,512]{1,0:T(8,128)(2,1)S(1)} %get-tuple-element.15), channel_id=1, source_target_pairs={{32,0},{64,32},{96,64},{128,96},{160,128},{192,160},{224,192},{256... | collective-permute-start | bytes 393224 | tf_op jit(solution)/shard_map/ppermute | solution.py:28
  168.5 26.3 %collective-permute-start.4 = (bf16[1,256]{1,0:T(2,128)(2,1)S(1)}, bf16[1,256]{1,0:T(2,128)(2,1)S(1)}, u32[]{:S(2)}, u32[]{:S(2)}) collective-permute-start(bf16[1,256]{1,0:T(2,128)(2,1)S(1)} %get-tuple-element.32), channel_id=1, source_target_pairs={{0,32},{32,64},{64,96},{96,128},{128,160},{160,192},{192,224},{224... | collective-permute-start | bytes 1544 | tf_op jit(solution)/shard_map/ppermute | solution.py:25
  192.9 25.9 %collective-permute-start.5 = (bf16[1,256]{1,0:T(2,128)(2,1)S(1)}, bf16[1,256]{1,0:T(2,128)(2,1)S(1)}, u32[]{:S(2)}, u32[]{:S(2)}) collective-permute-start(bf16[1,256]{1,0:T(2,128)(2,1)S(1)} %get-tuple-element.33), channel_id=1, source_target_pairs={{32,0},{64,32},{96,64},{128,96},{160,128},{192,160},{224,192},{256... | collective-permute-start | bytes 1544 | tf_op jit(solution)/shard_map/ppermute | solution.py:28
  218.9 14.9 %collective-permute-start.10 = (bf16[768,128]{1,0:T(8,128)(2,1)S(1)}, bf16[768,128]{1,0:T(8,128)(2,1)S(1)}, u32[]{:S(2)}, u32[]{:S(2)}) collective-permute-start(bf16[768,128]{1,0:T(8,128)(2,1)S(1)} %get-tuple-element.8), channel_id=1, source_target_pairs={{0,2},{2,4},{4,6},{6,8},{8,10},{10,12},{12,14},{14,16},{16,18},{18... | collective-permute-start | bytes 589832 | tf_op jit(solution)/shard_map/ppermute | solution.py:25
  221.5 12.3 %collective-permute-start.11 = (bf16[768,128]{1,0:T(8,128)(2,1)S(1)}, bf16[768,128]{1,0:T(8,128)(2,1)S(1)}, u32[]{:S(2)}, u32[]{:S(2)}) collective-permute-start(bf16[768,128]{1,0:T(8,128)(2,1)S(1)} %get-tuple-element.9), channel_id=1, source_target_pairs={{2,0},{4,2},{6,4},{8,6},{10,8},{12,10},{14,12},{16,14},{18,16},{20... | collective-permute-start | bytes 589832 | tf_op jit(solution)/shard_map/ppermute | solution.py:28
  222.8 6.5 %collective-permute-start.6 = (bf16[258,1]{1,0:T(8,128)(2,1)S(1)}, bf16[258,1]{1,0:T(8,128)(2,1)S(1)}, u32[]{:S(2)}, u32[]{:S(2)}) collective-permute-start(bf16[258,1]{1,0:T(8,128)(2,1)S(1)} %get-tuple-element.26), channel_id=1, source_target_pairs={{0,2},{2,4},{4,6},{6,8},{8,10},{10,12},{12,14},{14,16},{16,18},{18... | collective-permute-start | bytes 1556 | tf_op jit(solution)/shard_map/ppermute | solution.py:25
  227.4 6.2 %collective-permute-start.7 = (bf16[258,1]{1,0:T(8,128)(2,1)S(1)}, bf16[258,1]{1,0:T(8,128)(2,1)S(1)}, u32[]{:S(2)}, u32[]{:S(2)}) collective-permute-start(bf16[258,1]{1,0:T(8,128)(2,1)S(1)} %get-tuple-element.27), channel_id=1, source_target_pairs={{2,0},{4,2},{6,4},{8,6},{10,8},{12,10},{14,12},{16,14},{18,16},{20... | collective-permute-start | bytes 1556 | tf_op jit(solution)/shard_map/ppermute | solution.py:28
  233.8 0.7 copy-start.2
  234.5 0.9 copy-start
  235.9 5.9 %collective-permute-start.12 = (bf16[1,256]{1,0:T(2,128)(2,1)S(1)}, bf16[1,256]{1,0:T(2,128)(2,1)S(1)}, u32[]{:S(2)}, u32[]{:S(2)}) collective-permute-start(bf16[1,256]{1,0:T(2,128)(2,1)S(1)} %get-tuple-element.30), channel_id=1, source_target_pairs={{0,32},{32,64},{64,96},{96,128},{128,160},{160,192},{192,224},{224... | collective-permute-start | bytes 1544 | tf_op jit(solution)/shard_map/ppermute | solution.py:25
  237.8 25.9 %collective-permute-start.13 = (bf16[1,256]{1,0:T(2,128)(2,1)S(1)}, bf16[1,256]{1,0:T(2,128)(2,1)S(1)}, u32[]{:S(2)}, u32[]{:S(2)}) collective-permute-start(bf16[1,256]{1,0:T(2,128)(2,1)S(1)} %get-tuple-element.31), channel_id=1, source_target_pairs={{32,0},{64,32},{96,64},{128,96},{160,128},{192,160},{224,192},{256... | collective-permute-start | bytes 1544 | tf_op jit(solution)/shard_map/ppermute | solution.py:28
  263.8 4.5 %collective-permute-start.14 = (bf16[258,1]{1,0:T(8,128)(2,1)S(1)}, bf16[258,1]{1,0:T(8,128)(2,1)S(1)}, u32[]{:S(2)}, u32[]{:S(2)}) collective-permute-start(bf16[258,1]{1,0:T(8,128)(2,1)S(1)} %get-tuple-element.24), channel_id=1, source_target_pairs={{0,2},{2,4},{4,6},{6,8},{8,10},{10,12},{12,14},{14,16},{16,18},{18... | collective-permute-start | bytes 1556 | tf_op jit(solution)/shard_map/ppermute | solution.py:25
  266.4 6.2 %collective-permute-start.15 = (bf16[258,1]{1,0:T(8,128)(2,1)S(1)}, bf16[258,1]{1,0:T(8,128)(2,1)S(1)}, u32[]{:S(2)}, u32[]{:S(2)}) collective-permute-start(bf16[258,1]{1,0:T(8,128)(2,1)S(1)} %get-tuple-element.25), channel_id=1, source_target_pairs={{2,0},{4,2},{6,4},{8,6},{10,8},{12,10},{14,12},{16,14},{18,16},{20... | collective-permute-start | bytes 1556 | tf_op jit(solution)/shard_map/ppermute | solution.py:28
  273.2 5.9 %collective-permute-start.16 = (bf16[1,256]{1,0:T(2,128)(2,1)S(1)}, bf16[1,256]{1,0:T(2,128)(2,1)S(1)}, u32[]{:S(2)}, u32[]{:S(2)}) collective-permute-start(bf16[1,256]{1,0:T(2,128)(2,1)S(1)} %get-tuple-element.28), channel_id=1, source_target_pairs={{0,32},{32,64},{64,96},{96,128},{128,160},{160,192},{192,224},{224... | collective-permute-start | bytes 1544 | tf_op jit(solution)/shard_map/ppermute | solution.py:25
  275.1 25.9 %collective-permute-start.17 = (bf16[1,256]{1,0:T(2,128)(2,1)S(1)}, bf16[1,256]{1,0:T(2,128)(2,1)S(1)}, u32[]{:S(2)}, u32[]{:S(2)}) collective-permute-start(bf16[1,256]{1,0:T(2,128)(2,1)S(1)} %get-tuple-element.29), channel_id=1, source_target_pairs={{32,0},{64,32},{96,64},{128,96},{160,128},{192,160},{224,192},{256... | collective-permute-start | bytes 1544 | tf_op jit(solution)/shard_map/ppermute | solution.py:28
  301.1 5.6 %collective-permute-start.18 = (bf16[258,1]{1,0:T(8,128)(2,1)S(1)}, bf16[258,1]{1,0:T(8,128)(2,1)S(1)}, u32[]{:S(2)}, u32[]{:S(2)}) collective-permute-start(bf16[258,1]{1,0:T(8,128)(2,1)S(1)} %get-tuple-element.22), channel_id=1, source_target_pairs={{0,2},{2,4},{4,6},{6,8},{8,10},{10,12},{12,14},{14,16},{16,18},{18... | collective-permute-start | bytes 1556 | tf_op jit(solution)/shard_map/ppermute | solution.py:25
  304.8 6.2 %collective-permute-start.19 = (bf16[258,1]{1,0:T(8,128)(2,1)S(1)}, bf16[258,1]{1,0:T(8,128)(2,1)S(1)}, u32[]{:S(2)}, u32[]{:S(2)}) collective-permute-start(bf16[258,1]{1,0:T(8,128)(2,1)S(1)} %get-tuple-element.23), channel_id=1, source_target_pairs={{2,0},{4,2},{6,4},{8,6},{10,8},{12,10},{14,12},{16,14},{18,16},{20... | collective-permute-start | bytes 1556 | tf_op jit(solution)/shard_map/ppermute | solution.py:28
Sparse Core Ops, SparseCore 0:
  95.8 40.7 all-reduce.4
where the time goes:
time: 320 us; the launch traced here: 319 us
  waiting for transfers between devices  150 us (47%)
  starting transfers between devices  126 us (39%)
  matrix products  17.6 us (6%)
  between operations  15.2 us (5%)
  other arithmetic  6.35 us (2%)
  local copies, waits for them, and re-layouts  3.78 us (1%)
    ppermute x10, waiting for transfers between devices, with_halo(): lax.ppermute(lax.slice_in_dim(block, 0, width, axis=dim), axis, backward)  107 us
    ppermute x10, starting transfers between devices, with_halo(): lax.ppermute(lax.slice_in_dim(block, block.shape[dim] - width, None, axis...  106 us
    psum x1, waiting for transfers between devices, body(): lax.psum(grad_spec_im.astype(jnp.bfloat16), 'corner').astype(jnp.float32)  40.9 us
    ppermute x10, starting transfers between devices, with_halo(): lax.ppermute(lax.slice_in_dim(block, 0, width, axis=dim), axis, backward)  20.1 us
    dot_general x9, matrix products, matmul(): return jnp.dot(left, right, preferred_element_type=jnp.float32)  11.6 us
  transfers between devices with their start and end apart: 21, of which 13 were waited for; matrix products, arithmetic and copies ran while one was open for 1% of the time, Pallas kernels for 0%

commit v1 on v0

v1 whole, which is shorter than its diff:
```python
import math

import jax
import jax.numpy as jnp
import ml_dtypes
import numpy as np
from jax import lax
from jax.experimental import pallas as pl
from jax.experimental.pallas import tpu as pltpu
from jax.sharding import PartitionSpec as P

TILE = 256
HALO = 128
KF = 128
WIN = 512
KERNELS = 5
LS_STEPS = 3

STEEPNESS = 4.0
THRESHOLD = 1.0
SPEED_GAIN = 4.0
SMOOTHING = 0.24
GRAD_FLOOR = 0.25

MESH = pl.DeviceIdType.MESH
F32 = jnp.float32
BF16 = jnp.bfloat16

EXT = 144
LANES = 384


def wide_tables():
    shifts = np.arange(KF, dtype=np.int32) - KF // 2
    places = np.arange(WIN, dtype=np.int32)
    phases = (shifts[:, None] * places[None, :]) % WIN
    angles = np.float32(2.0 * math.pi / WIN) * phases.astype(np.float32)
    scaled = np.float32(1.0 / math.sqrt(WIN))
    fc = np.cos(angles, dtype=np.float32) * scaled
    fs = -np.sin(angles, dtype=np.float32) * scaled
    inner = angles[:, HALO : HALO + TILE].T
    ic = np.cos(inner, dtype=np.float32) * scaled
    isn = np.sin(inner, dtype=np.float32) * scaled
    fwd = np.concatenate([fc, fs], 0)
    turn = np.concatenate([-fs, fc], 0)
    to_field = np.concatenate(
        [np.concatenate([ic.T, isn.T], 1), np.concatenate([-isn.T, ic.T], 1)], 0
    )
    inv = np.concatenate([ic, isn], 1)
    ft = fwd.T
    lo, hi = HALO, HALO + 128
    own = [
        np.concatenate([ft[lo:hi], ft[hi : hi + 8], ft[lo - 8 : lo]], 0),
        np.concatenate([ft[hi : hi + 128], ft[hi + 128 : hi + 136], ft[hi - 8 : hi]], 0),
    ]
    strip = [ft[368:512], np.concatenate([ft[128:144], ft[0:128]], 0)]
    cross = [
        np.concatenate([fwd[:, 384:512], fwd[:, 256:384]], 1),
        fwd[:, 0:256],
    ]
    a = np.concatenate([fwd, turn, to_field], 0)
    b = np.concatenate([ft, inv, to_field.T, inv.T] + own + strip + cross, 0)
    return a.astype(ml_dtypes.bfloat16), b.astype(ml_dtypes.bfloat16)


A_FWD, A_TURN, A_FIELD, A_ROWS = 0, 256, 512, 768
B_FT, B_INV, B_BACK, B_INVT, B_OWN = 0, 512, 768, 1280, 1536
B_STRIP = B_OWN + 2 * EXT
B_CROSS = B_STRIP + 2 * EXT
B_ROWS = B_CROSS + 512


def mm(x, y):
    return jnp.dot(x, y, preferred_element_type=F32)


def mm_nt(x, y):
    return lax.dot_general(x, y, (((1,), (1,)), ((), ())), preferred_element_type=F32)


def one_hot(shape, pairs):
    rows = lax.broadcasted_iota(jnp.int32, shape, 0)
    cols = lax.broadcasted_iota(jnp.int32, shape, 1)
    hit = jnp.zeros(shape, F32)
    for r, c in pairs:
        hit = jnp.where((rows == r) & (cols == c), 1.0, hit)
    return hit.astype(BF16)


def kernel(
    n_ty,
    n_tx,
    level_hbm,
    target_hbm,
    kern_hbm,
    dose_ref,
    a_hbm,
    b_hbm,
    resist_hbm,
    out_hbm,
    level_i,
    target_i,
    kern,
    ta,
    tb,
    win,
    trw,
    spec,
    fields,
    inten,
    sens2,
    resist,
    gacc,
    gother,
    hbuf,
    lift,
    glift,
    msg_s,
    msg_r,
    small_s,
    small_r,
    final,
    in_sem,
    out_sem,
    send,
    s_side,
    s_far,
    s_fan,
    s_part,
    s_corner,
    s_spec,
    s_msg,
    s_small,
    s_final,
):
    a, b, c = lax.axis_index("ty"), lax.axis_index("tx"), lax.axis_index("corner")
    has_l, has_r = b > 0, b < n_tx - 1
    up_ok, dn_ok = a > 0, a < n_ty - 1
    is0 = c == 0
    send_ok = jnp.where(is0, dn_ok.astype(jnp.int32), up_ok.astype(jnp.int32)) > 0
    recv_ok = jnp.where(is0, up_ok.astype(jnp.int32), dn_ok.astype(jnp.int32)) > 0
    ar = a + 1 - 2 * c
    bl, br = jnp.maximum(b - 1, 0), jnp.minimum(b + 1, n_tx - 1)
    zl, zr = jnp.where(has_l, 0, 1), jnp.where(has_r, 0, 1)
    other = 1 - c
    left, right, partner = (a, b - 1, c), (a, b + 1, c), (a, b, other)

    def local(src, dst, sem):
        cp = pltpu.make_async_copy(src, dst, sem)
        cp.start()
        return cp

    def remote(i, src, dst, rsem, dev):
        return pltpu.make_async_remote_copy(
            src_ref=src,
            dst_ref=dst,
            send_sem=send.at[i],
            recv_sem=rsem,
            device_id=dev,
            device_id_type=MESH,
        )

    def arrived(dst, rsem):
        pltpu.make_async_remote_copy(
            src_ref=dst,
            dst_ref=dst,
            send_sem=send.at[0],
            recv_sem=rsem,
            device_id=partner,
            device_id_type=MESH,
        ).wait_recv()

    cp_level = local(level_hbm, level_i, in_sem.at[0])
    cp_a = local(a_hbm, ta, in_sem.at[1])
    cp_kern = local(kern_hbm, kern, in_sem.at[2])
    cp_b = local(b_hbm, tb, in_sem.at[3])
    cp_target = local(target_hbm, target_i, in_sem.at[4])

    barrier = pltpu.get_barrier_semaphore()

    def hello(dev):
        pl.semaphore_signal(barrier, inc=1, device_id=dev, device_id_type=MESH)

    @pl.when(up_ok)
    def _():
        hello((a - 1, bl, 0))
        hello((a - 1, br, 0))

    @pl.when(dn_ok)
    def _():
        hello((a + 1, bl, 1))
        hello((a + 1, br, 1))

    hello(partner)

    @pl.when(has_l)
    def _():
        hello((a, b - 1, 0))
        hello((a, b - 1, 1))

    @pl.when(has_r)
    def _():
        hello((a, b + 1, 0))
        hello((a, b + 1, 1))

    cp_level.wait()
    level0 = level_i[...].astype(F32) * 0.125
    low = level0.astype(BF16)
    win[1, 128:384] = low[:, :128]
    win[2, 128:384] = low[:, 128:]

    wanted = (
        1
        + 2 * has_l.astype(jnp.int32)
        + 2 * has_r.astype(jnp.int32)
        + 4 * send_ok.astype(jnp.int32)
    )
    pl.semaphore_wait(barrier, wanted)

    srow = pl.multiple_of(256 - 128 * c, 128)
    hrow = pl.multiple_of(384 * c, 128)
    fl = remote(0, win.at[1, pl.ds(srow, 128)], win.at[jnp.where(has_l, 3, 1), pl.ds(hrow, 128)], s_far.at[1 - zl], (ar, bl, c))
    fr = remote(1, win.at[2, pl.ds(srow, 128)], win.at[jnp.where(has_r, 0, 2), pl.ds(hrow, 128)], s_far.at[zr], (ar, br, c))
    sl = remote(2, win.at[1, pl.ds(128, 256)], win.at[3, pl.ds(128, 256)], s_side.at[1], left)
    sr = remote(3, win.at[2, pl.ds(128, 256)], win.at[0, pl.ds(128, 256)], s_side.at[0], right)

    @pl.when(send_ok)
    def _():
        fl.start()
        fr.start()

    @pl.when(has_l)
    def _():
        sl.start()

    @pl.when(has_r)
    def _():
        sr.start()

    @pl.when(jnp.logical_not(has_l))
    def _():
        win[0] = jnp.zeros((WIN, 128), BF16)
        hbuf[0] = jnp.zeros((KF, 256), BF16)

    @pl.when(jnp.logical_not(has_r))
    def _():
        win[3] = jnp.zeros((WIN, 128), BF16)
        hbuf[2] = jnp.zeros((KF, 256), BF16)

    for q, ok in ((0, up_ok), (384, dn_ok)):
        @pl.when(jnp.logical_not(ok))
        def _(q=q):
            for blk in range(4):
                win[blk, q : q + 128] = jnp.zeros((128, 128), BF16)

    @pl.when(jnp.logical_not(recv_ok))
    def _():
        msg_r[...] = jnp.zeros_like(msg_r)

    small_ok = jnp.where(is0, dn_ok.astype(jnp.int32), up_ok.astype(jnp.int32)) > 0

    @pl.when(jnp.logical_not(small_ok))
    def _():
        small_r[...] = jnp.zeros_like(small_r)

    def to_trans(blk, r0, rows):
        x = win[blk, r0 : r0 + rows].astype(F32)
        trw[r0 : r0 + rows, blk * 128 : blk * 128 + 128] = jnp.tanh(0.25 * x).astype(BF16)

    to_trans(1, 128, 256)
    to_trans(2, 128, 256)

    @pl.when(has_l)
    def _():
        arrived(win.at[0, pl.ds(128, 256)], s_side.at[0])

    to_trans(0, 128, 256)

    @pl.when(has_r)
    def _():
        arrived(win.at[3, pl.ds(128, 256)], s_side.at[1])

    to_trans(3, 128, 256)
    cp_a.wait()
    cp_b.wait()
    cp_kern.wait()
    cp_target.wait()
    lift[...] = mm(ta[A_FWD : A_FWD + 256, 128:384], trw[128:384, :])

    blk_l, blk_r = jnp.where(has_l, 0, 1), jnp.where(has_r, 3, 2)
    got_l, got_r = win.at[blk_l, pl.ds(hrow, 128)], win.at[blk_r, pl.ds(hrow, 128)]
    pl_ = remote(4, got_l, got_l, s_part.at[0], partner)
    pr_ = remote(5, got_r, got_r, s_part.at[1], partner)
    fan_l = [remote(6 + d, got_l, win.at[2, pl.ds(hrow, 128)], s_fan.at[c, 1], (a, b - 1, d)) for d in (0, 1)]
    fan_r = [remote(8 + d, got_r, win.at[1, pl.ds(hrow, 128)], s_fan.at[c, 0], (a, b + 1, d)) for d in (0, 1)]

    @pl.when(recv_ok)
    def _():
        arrived(got_l, s_far.at[0])

        @pl.when(has_l)
        def _():
            fan_l[0].start()
            fan_l[1].start()

        pl_.start()
        arrived(got_r, s_far.at[1])

        @pl.when(has_r)
        def _():
            fan_r[0].start()
            fan_r[1].start()

        pr_.start()

    @pl.when(small_ok)
    def _():
        orow = pl.multiple_of(384 * other, 128)
        arrived(win.at[blk_l, pl.ds(orow, 128)], s_part.at[0])
        arrived(win.at[blk_r, pl.ds(orow, 128)], s_part.at[1])

    for d, ok in ((0, up_ok), (1, dn_ok)):
        @pl.when(ok & has_l)
        def _(d=d):
            arrived(win.at[1, pl.ds(384 * d, 128)], s_fan.at[d, 0])

        @pl.when(ok & has_r)
        def _(d=d):
            arrived(win.at[2, pl.ds(384 * d, 128)], s_fan.at[d, 1])

    for blk in range(4):
        to_trans(blk, 0, 128)
        to_trans(blk, 384, 128)
    lift_b = (
        lift[...]
        + mm(ta[A_FWD : A_FWD + 256, 0:128], trw[0:128, :])
        + mm(ta[A_FWD : A_FWD + 256, 384:512], trw[384:512, :])
    ).astype(BF16)
    s = mm(lift_b, tb[B_FT : B_FT + 512])
    spec[0] = s[:128, :128] - s[128:, 128:]
    spec[1] = s[:128, 128:] + s[128:, :128]

    dose = dose_ref[0]
    inten[...] = jnp.zeros_like(inten)

    def ahead(k, _):
        kr, ki = kern[0, k, 0], kern[0, k, 1]
        sre, sim = spec[0], spec[1]
        bre = (kr * sre - ki * sim).astype(BF16)
        bim = (kr * sim + ki * sre).astype(BF16)
        blur = jnp.concatenate(
            [jnp.concatenate([bre, bim], 1), jnp.concatenate([-bim, bre], 1)], 0
        )
        proj = mm(tb[B_INV : B_INV + 256], blur).astype(BF16)
        field = mm(proj, ta[A_FIELD : A_FIELD + 256])
        fields[k] = field
        fre, fim = field[:, :256], field[:, 256:]
        inten[...] += fre * fre + fim * fim
        return 0

    lax.fori_loop(0, KERNELS, ahead, 0)

    res = jax.nn.sigmoid(STEEPNESS * (dose * inten[...] - THRESHOLD))
    resist[...] = res
    cp_resist = local(resist, resist_hbm.at[0], out_sem.at[0])
    goal = target_i[...].astype(F32)
    sens2[...] = 2.0 * (2.0 * (res - goal) * STEEPNESS * dose * res * (1.0 - res))
    gacc[...] = jnp.zeros_like(gacc)

    def back(k, _):
        kr, ki = kern[0, k, 0], kern[0, k, 1]
        s2 = sens2[...]
        adj = (jnp.concatenate([s2, s2], 1) * fields[k]).astype(BF16)
        bk = mm(adj, tb[B_BACK : B_BACK + 512]).astype(BF16)
        g = mm(tb[B_INVT : B_INVT + 256], bk)
        gre = g[:128, :128] + g[128:, 128:]
        gim = g[:128, 128:] - g[128:, :128]
        gacc[:, :128] += kr * gre + ki * gim
        gacc[:, 128:] += kr * gim - ki * gre
        return 0

    lax.fori_loop(0, KERNELS, back, 0)

    cc = remote(10, gacc, gother, s_corner, partner)
    cc.start()
    arrived(gother, s_corner)
    hbuf[1] = (gacc[...] + gother[...]).astype(BF16)
    hl = remote(11, hbuf.at[1], hbuf.at[2], s_spec.at[1], left)
    hr = remote(12, hbuf.at[1], hbuf.at[0], s_spec.at[0], right)

    @pl.when(has_l)
    def _():
        hl.start()

    @pl.when(has_r)
    def _():
        hr.start()

    glift[0:128] = mm(hbuf[1], ta[A_FWD : A_FWD + 256])
    glift[128:256] = mm(hbuf[1], ta[A_TURN : A_TURN + 256])

    rows0 = pl.multiple_of(128 + 128 * c, 128)
    below = pl.multiple_of(256 + 128 * c, 128)
    above = pl.multiple_of(112 + 128 * c, 16)
    lane = lax.broadcasted_iota(jnp.int32, (EXT, 128), 1)

    def level_rows(blk):
        main = win[blk, pl.ds(rows0, 128)].astype(F32)
        after = win[blk, pl.ds(below, 16)].astype(F32)[0:8]
        before = win[blk, pl.ds(above, 16)].astype(F32)[8:16]
        return jnp.concatenate([main, after, before], 0)

    def ring(x, y):
        return jnp.where(lane < 64, x, y)

    level = jnp.concatenate([level_rows(1), level_rows(2), ring(level_rows(3), level_rows(0))], 1)
    trans = jnp.tanh(0.25 * level)
    final[:, 0:LANES] = level
    final[:, LANES : 2 * LANES] = 0.25 * (1.0 - trans * trans)

    @pl.when(has_l)
    def _():
        arrived(hbuf.at[0], s_spec.at[0])

    @pl.when(has_r)
    def _():
        arrived(hbuf.at[2], s_spec.at[1])

    for r, q in ((0, A_FWD), (128, A_TURN)):
        glift[r : r + 128, 0:256] += mm(hbuf[0], ta[q : q + 256, 256:512])
        glift[r : r + 128, 256:512] += mm(hbuf[2], ta[q : q + 256, 0:256])
    gl = glift[...].astype(BF16)

    gblk = [glift[:, 128 * i : 128 * i + 128] for i in range(4)]
    out_l = jnp.where(has_l, gblk[0], gblk[1]).astype(BF16)
    out_r = jnp.where(has_r, gblk[3], gblk[2]).astype(BF16)
    strip = mm(tb[pl.ds(pl.multiple_of(B_STRIP + EXT * c, 16), EXT)], jnp.concatenate([out_l, out_r], 1))
    pick_l = one_hot((16, 128), [(0, 0), (1, 1), (2, 0), (3, 1)])
    pick_r = one_hot((16, 128), [(0, 126), (1, 127), (2, 126), (3, 127)])
    picked = jnp.concatenate([mm_nt(pick_l, gl[:, 128:256]), mm_nt(pick_r, gl[:, 256:384])], 0)
    crossed = mm(picked.astype(BF16), tb[pl.ds(pl.multiple_of(B_CROSS + 256 * c, 16), 256)])
    row16 = lax.broadcasted_iota(jnp.int32, (16, 128), 0)
    for side in range(2):
        cols = slice(128 * side, 128 * side + 128)
        cr = crossed[16 * side : 16 * side + 16]
        edge = jnp.where(row16 < 2, cr[:, :128], cr[:, 128:]).astype(BF16)
        part = strip[:, cols]
        msg_s[side, 0:16] = edge
        msg_s[side, 16:160] = part.astype(BF16)
        small_s[side, 0:16] = edge
        small_s[side, 16:32] = jnp.where(is0, part[128:144], part[16:32]).astype(BF16)

    ml = remote(13, msg_s.at[0], msg_r.at[1 - zl], s_msg.at[1 - zl], (ar, bl, c))
    mr = remote(14, msg_s.at[1], msg_r.at[zr], s_msg.at[zr], (ar, br, c))
    nl = remote(15, small_s.at[0], small_r.at[1 - zl], s_small.at[1 - zl], (ar, bl, other))
    nr = remote(16, small_s.at[1], small_r.at[zr], s_small.at[zr], (ar, br, other))

    @pl.when(send_ok)
    def _():
        ml.start()
        mr.start()
        nl.start()
        nr.start()

    ring_lane = lax.broadcasted_iota(jnp.int32, (256, 128), 1)
    gl_ring = jnp.where(ring_lane < 64, gblk[3], gblk[0]).astype(BF16)
    own_rows = tb[pl.ds(pl.multiple_of(B_OWN + EXT * c, 16), EXT)]
    grad = mm(own_rows, jnp.concatenate([gl[:, 128:384], gl_ring], 1))

    @pl.when(recv_ok)
    def _():
        arrived(msg_r.at[0], s_msg.at[0])
        arrived(msg_r.at[1], s_msg.at[1])

    @pl.when(small_ok)
    def _():
        arrived(small_r.at[0], s_small.at[0])
        arrived(small_r.at[1], s_small.at[1])

    eye = one_hot((128, 128), [])
    r128 = lax.broadcasted_iota(jnp.int32, (128, 128), 0)
    c128 = lax.broadcasted_iota(jnp.int32, (128, 128), 1)
    eye = jnp.where(r128 == c128, 1.0, 0.0).astype(BF16)
    sel_a = one_hot((32, 128), [(0, 126), (1, 127), (16, 0), (17, 1)])
    sel_b = one_hot((32, 128), [(2, 126), (3, 127), (18, 0), (19, 1)])
    edges = jnp.concatenate([msg_r[0, 0:16], msg_r[1, 0:16]], 0)
    edges_s = jnp.concatenate([small_r[0, 0:16], small_r[1, 0:16]], 0)
    turned = mm_nt(eye, edges).astype(BF16)
    turned_s = mm_nt(eye, edges_s).astype(BF16)
    col_main = mm(turned, sel_a)
    col_far = mm(turned, sel_b)
    col_small = mm(turned_s, sel_a)

    def add_part(blocks_main, blocks_ext, blocks_small):
        main = jnp.concatenate(blocks_main, 1)
        far = jnp.concatenate(blocks_ext, 1)
        near = jnp.concatenate(blocks_small, 1)
        after = jnp.where(is0, near[0:8], far[0:8])
        before = jnp.where(is0, far[8:16], near[8:16])
        return jnp.concatenate([main, after, before], 0)

    col_far16 = jnp.concatenate([col_far[0:8], col_far[120:128]], 0)
    col_small16 = jnp.concatenate([col_small[0:8], col_small[120:128]], 0)
    received = add_part(
        [msg_r[0, 32:160].astype(F32), msg_r[1, 32:160].astype(F32), col_main],
        [msg_r[0, 16:32].astype(F32), msg_r[1, 16:32].astype(F32), col_far16],
        [small_r[0, 16:32].astype(F32), small_r[1, 16:32].astype(F32), col_small16],
    )
    speed = SPEED_GAIN * (grad + received) * final[:, LANES : 2 * LANES]

    row = lax.broadcasted_iota(jnp.int32, (EXT, LANES), 0)
    col = lax.broadcasted_iota(jnp.int32, (EXT, LANES), 1)
    i_off = jnp.where(row < 136, row, row - EXT) + 128 * c
    j_off = jnp.where(col < 320, col, col - LANES)
    i_all = a * TILE + i_off
    j_all = b * TILE + j_off
    inside = (i_all >= 0) & (i_all < n_ty * TILE) & (j_all >= 0) & (j_all < n_tx * TILE)

    level = final[:, 0:LANES]
    for _ in range(LS_STEPS):
        up = pltpu.roll(level, 1, 0)
        down = pltpu.roll(level, EXT - 1, 0)
        lf = pltpu.roll(level, 1, 1)
        rt = pltpu.roll(level, LANES - 1, 1)
        sy = 0.5 * (down - up)
        sx = 0.5 * (rt - lf)
        spread = up + down + lf + rt - 4.0 * level
        level = level - speed * jnp.sqrt(GRAD_FLOOR + sy * sy + sx * sx) + SMOOTHING * spread
        level = jnp.where(inside, level, 0.0)
    final[0:128, 0:256] = level[0:128, 0:256]

    mine = out_hbm.at[pl.ds(pl.multiple_of(128 * c, 128), 128)]
    result = final.at[pl.ds(0, 128), pl.ds(0, 256)]
    ff = remote(17, result, mine, s_final, partner)
    ff.start()
    cp_out = local(result, mine, out_sem.at[1])

    cp_resist.wait()
    cp_out.wait()

    @pl.when(send_ok)
    def _():
        for d in (fl, fr, ml, mr, nl, nr):
            d.wait_send()

    @pl.when(has_l)
    def _():
        sl.wait_send()
        hl.wait_send()

    @pl.when(has_r)
    def _():
        sr.wait_send()
        hr.wait_send()

    @pl.when(recv_ok)
    def _():
        pl_.wait_send()
        pr_.wait_send()

    @pl.when(recv_ok & has_l)
    def _():
        fan_l[0].wait_send()
        fan_l[1].wait_send()

    @pl.when(recv_ok & has_r)
    def _():
        fan_r[0].wait_send()
        fan_r[1].wait_send()

    cc.wait_send()
    ff.wait_send()
    arrived(out_hbm.at[pl.ds(pl.multiple_of(128 * other, 128), 128)], s_final)


def make_body(n_ty, n_tx):
    def body(level_init, target, kernels, corner_doses):
        ta, tb = wide_tables()
        dma = pltpu.SemaphoreType.DMA
        anywhere = pl.BlockSpec(memory_space=pl.ANY)

        def whole(*args):
            return kernel(n_ty, n_tx, *args)

        return pl.pallas_call(
            whole,
            out_shape=(
                jax.ShapeDtypeStruct((1, TILE, TILE), F32),
                jax.ShapeDtypeStruct((TILE, TILE), F32),
            ),
            in_specs=[
                anywhere,
                anywhere,
                anywhere,
                pl.BlockSpec(memory_space=pltpu.SMEM),
                anywhere,
                anywhere,
            ],
            out_specs=(anywhere, anywhere),
            scratch_shapes=[
                pltpu.VMEM((TILE, TILE), jnp.int32),
                pltpu.VMEM((TILE, TILE), jnp.int32),
                pltpu.VMEM((1, KERNELS, 2, KF, KF), F32),
                pltpu.VMEM((A_ROWS, 512), BF16),
                pltpu.VMEM((B_ROWS, 256), BF16),
                pltpu.VMEM((4, WIN, 128), BF16),
                pltpu.VMEM((WIN, WIN), BF16),
                pltpu.VMEM((2, KF, KF), F32),
                pltpu.VMEM((KERNELS, TILE, 2 * TILE), F32),
                pltpu.VMEM((TILE, TILE), F32),
                pltpu.VMEM((TILE, TILE), F32),
                pltpu.VMEM((TILE, TILE), F32),
                pltpu.VMEM((KF, 2 * KF), F32),
                pltpu.VMEM((KF, 2 * KF), F32),
                pltpu.VMEM((3, KF, 2 * KF), BF16),
                pltpu.VMEM((2 * KF, WIN), F32),
                pltpu.VMEM((2 * KF, WIN), F32),
                pltpu.VMEM((2, 160, 128), BF16),
                pltpu.VMEM((2, 160, 128), BF16),
                pltpu.VMEM((2, 32, 128), BF16),
                pltpu.VMEM((2, 32, 128), BF16),
                pltpu.VMEM((EXT, 2 * LANES), F32),
                dma((5,)),
                dma((2,)),
                dma((18,)),
                dma((2,)),
                dma((2,)),
                dma((2, 2)),
                dma((2,)),
                dma,
                dma((2,)),
                dma((2,)),
                dma((2,)),
                dma,
            ],
            compiler_params=pltpu.CompilerParams(
                collective_id=0,
                has_side_effects=True,
                vmem_limit_bytes=62 * 1024 * 1024,
            ),
            cost_estimate=pl.CostEstimate(
                flops=1_500_000_000, bytes_accessed=6_000_000, transcendentals=400_000
            ),
        )(level_init, target, kernels, corner_doses, jnp.asarray(ta), jnp.asarray(tb))

    return body


def solution(mesh):
    in_specs = (P("ty", "tx"), P("ty", "tx"), P("corner", None, None, None, None), P("corner"))
    out_specs = (P("corner", "ty", "tx"), P("ty", "tx"))
    return jax.shard_map(
        make_body(mesh.shape["ty"], mesh.shape["tx"]),
        mesh=mesh,
        in_specs=in_specs,
        out_specs=out_specs,
        check_vma=False,
    )
```

time: 320 us -> 83 us (0.26)
  the two profiles are of different devices: /device:TPU:24 before, /device:TPU:7 now
where the time goes in v1:
time: 83 us; the launch traced here: 82.8 us
  Pallas kernels  78.2 us (94%)
  local copies, waits for them, and re-layouts  3.34 us (4%)
  between operations  1.29 us (2%)
    pallas_call x1, Pallas kernels, body(): pl.pallas_call(whole, out_shape=(jax.ShapeDtypeStruct((1, TILE, TILE), F3...  78.2 us
    unnamed x2, local copies, waits for them, and re-layouts  3.34 us

profile of v1, /device:TPU:7, one launch (start us, length us, event | category | flops | bytes accessed | tf_op | source)
XLA Modules:
  0.0 82.8 jit_solution(4554523412227643897)
XLA Ops:
  1.3 78.2 %shard_map.77 = (f32[1,256,256]{2,1,0:T(8,128)}, f32[256,256]{1,0:T(8,128)}) custom-call(s32[256,256]{1,0:T(8,128)} %args_0_.4, s32[256,256]{1,0:T(8,128)} %args_1_.4, f32[1,5,2,128,128]{4,3,2,1,0:T(8,128)} %args_2_.4, f32[1]{0:T(128)S(6)} %copy.10.args_3_, bf16[768,512]{1,0:T(8,128)(2,1)} %constant.4.clone.args_4_, bf16[2624,256]{1,0:T(8,128)(2,1)} %constant.5.clone.args_5_), custom_call_target="tpu_custom_call" | custom-call | flops 1500000000 | bytes 6000000 | tf_op jit(solution)/shard_map/pallas_call | solution.py:585
  79.5 1.7 %copy.11 = f32[1,256,256]{2,1,0:T(8,128)} copy(f32[1,256,256]{2,1,0:T(8,128)} %get-tuple-element.4) | data formatting | bytes 524288
  81.1 1.7 %copy.12 = f32[256,256]{1,0:T(8,128)} copy(f32[256,256]{1,0:T(8,128)} %get-tuple-element.5) | data formatting | bytes 524288

commit v2 on v1

--- a/solution.py
+++ b/solution.py
@@ -120,6 +120,7 @@
     small_s,
     small_r,
     final,
+    held,
     in_sem,
     out_sem,
     send,
@@ -132,6 +133,9 @@
     s_msg,
     s_small,
     s_final,
+    s_held,
+    ready,
+    ready_relay,
 ):
     a, b, c = lax.axis_index("ty"), lax.axis_index("tx"), lax.axis_index("corner")
     has_l, has_r = b > 0, b < n_tx - 1
@@ -143,6 +147,19 @@
     bl, br = jnp.maximum(b - 1, 0), jnp.minimum(b + 1, n_tx - 1)
     zl, zr = jnp.where(has_l, 0, 1), jnp.where(has_r, 0, 1)
     other = 1 - c
+
+    early_dn, early_up = (a % 8 == 3) & dn_ok, (a % 8 == 0) & up_ok
+    late_up, late_dn = (a % 8 == 4) & up_ok, (a % 8 == 7) & dn_ok
+    early, late = early_dn | early_up, late_up | late_dn
+    far_row = jnp.where(early_dn | late_dn, a + 1, a - 1)
+    far_core = jnp.where(early_dn | late_up, 0, 1)
+    hops = early & (c == far_core)
+    meets = late & (c == far_core)
+    half = n_tx // 2
+    bp = (b + half) % n_tx
+    bpl, bpr = jnp.maximum(bp - 1, 0), jnp.minimum(bp + 1, n_tx - 1)
+    zpl, zpr = jnp.where(bp > 0, 0, 1), jnp.where(bp < n_tx - 1, 0, 1)
+    straight = send_ok & jnp.logical_not(hops)
     left, right, partner = (a, b - 1, c), (a, b + 1, c), (a, b, other)
 
     def local(src, dst, sem):
@@ -181,15 +198,23 @@
     def hello(dev):
         pl.semaphore_signal(barrier, inc=1, device_id=dev, device_id_type=MESH)
 
-    @pl.when(up_ok)
+    @pl.when(up_ok & jnp.logical_not(late_up))
     def _():
         hello((a - 1, bl, 0))
         hello((a - 1, br, 0))
 
-    @pl.when(dn_ok)
+    @pl.when(dn_ok & jnp.logical_not(late_dn))
     def _():
         hello((a + 1, bl, 1))
         hello((a + 1, br, 1))
+
+    @pl.when(hops)
+    def _():
+        hello((a, bp, c))
+        hello((far_row, bl, c))
+        hello((far_row, br, c))
+        hello((far_row, bpl, c))
+        hello((far_row, bpr, c))
 
     hello(partner)
 
@@ -213,9 +238,26 @@
         1
         + 2 * has_l.astype(jnp.int32)
         + 2 * has_r.astype(jnp.int32)
-        + 4 * send_ok.astype(jnp.int32)
+        + 4 * straight.astype(jnp.int32)
+        + hops.astype(jnp.int32)
+        + 4 * meets.astype(jnp.int32)
     )
     pl.semaphore_wait(barrier, wanted)
+
+    @pl.when(late)
+    def _():
+        for to in (bl, br):
+            pl.semaphore_signal(ready, inc=1, device_id=(far_row, to, far_core), device_id_type=MESH)
+
+    @pl.when(meets)
+    def _():
+        for to in (bl, br):
+            pl.semaphore_signal(
+                ready_relay,
+                inc=1,
+                device_id=(far_row, (to + half) % n_tx, far_core),
+                device_id_type=MESH,
+            )
 
     srow = pl.multiple_of(256 - 128 * c, 128)
     hrow = pl.multiple_of(384 * c, 128)
@@ -224,10 +266,20 @@
     sl = remote(2, win.at[1, pl.ds(128, 256)], win.at[3, pl.ds(128, 256)], s_side.at[1], left)
     sr = remote(3, win.at[2, pl.ds(128, 256)], win.at[0, pl.ds(128, 256)], s_side.at[0], right)
 
-    @pl.when(send_ok)
+    kl = remote(18, win.at[1, pl.ds(srow, 128)], held.at[0], s_held.at[0], (a, bp, c))
+    kr_ = remote(19, win.at[2, pl.ds(srow, 128)], held.at[1], s_held.at[1], (a, bp, c))
+    ol = remote(20, held.at[0], win.at[jnp.where(bp > 0, 3, 1), pl.ds(hrow, 128)], s_far.at[1 - zpl], (far_row, bpl, c))
+    orr = remote(21, held.at[1], win.at[jnp.where(bp < n_tx - 1, 0, 2), pl.ds(hrow, 128)], s_far.at[zpr], (far_row, bpr, c))
+
+    @pl.when(straight)
     def _():
         fl.start()
         fr.start()
+
+    @pl.when(hops)
+    def _():
+        kl.start()
+        kr_.start()
 
     @pl.when(has_l)
     def _():
@@ -286,6 +338,14 @@
     cp_kern.wait()
     cp_target.wait()
     lift[...] = mm(ta[A_FWD : A_FWD + 256, 128:384], trw[128:384, :])
+
+    @pl.when(hops)
+    def _():
+        pl.semaphore_wait(ready_relay, 2)
+        arrived(held.at[0], s_held.at[0])
+        ol.start()
+        arrived(held.at[1], s_held.at[1])
+        orr.start()
 
     blk_l, blk_r = jnp.where(has_l, 0, 1), jnp.where(has_r, 3, 2)
     got_l, got_r = win.at[blk_l, pl.ds(hrow, 128)], win.at[blk_r, pl.ds(hrow, 128)]
@@ -443,17 +503,22 @@
     for side in range(2):
         cols = slice(128 * side, 128 * side + 128)
         cr = crossed[16 * side : 16 * side + 16]
-        edge = jnp.where(row16 < 2, cr[:, :128], cr[:, 128:]).astype(BF16)
+        edge = jnp.where(row16 < 2, cr[:, :128], cr[:, 128:])[0:8]
         part = strip[:, cols]
-        msg_s[side, 0:16] = edge
-        msg_s[side, 16:160] = part.astype(BF16)
-        small_s[side, 0:16] = edge
-        small_s[side, 16:32] = jnp.where(is0, part[128:144], part[16:32]).astype(BF16)
+        near_rows = jnp.where(is0, part[8:16], part[0:8])
+        msg_s[side, 0:16] = jnp.concatenate([edge, near_rows], 0).astype(BF16)
+        msg_s[side, 16:EXT] = part[16:EXT].astype(BF16)
+        tail_rows = jnp.where(is0, part[136:144], part[16:24])
+        small_s[side] = jnp.concatenate([edge, tail_rows], 0).astype(BF16)
 
     ml = remote(13, msg_s.at[0], msg_r.at[1 - zl], s_msg.at[1 - zl], (ar, bl, c))
     mr = remote(14, msg_s.at[1], msg_r.at[zr], s_msg.at[zr], (ar, br, c))
     nl = remote(15, small_s.at[0], small_r.at[1 - zl], s_small.at[1 - zl], (ar, bl, other))
     nr = remote(16, small_s.at[1], small_r.at[zr], s_small.at[zr], (ar, br, other))
+
+    @pl.when(hops)
+    def _():
+        pl.semaphore_wait(ready, 4)
 
     @pl.when(send_ok)
     def _():
@@ -484,7 +549,7 @@
     sel_a = one_hot((32, 128), [(0, 126), (1, 127), (16, 0), (17, 1)])
     sel_b = one_hot((32, 128), [(2, 126), (3, 127), (18, 0), (19, 1)])
     edges = jnp.concatenate([msg_r[0, 0:16], msg_r[1, 0:16]], 0)
-    edges_s = jnp.concatenate([small_r[0, 0:16], small_r[1, 0:16]], 0)
+    edges_s = jnp.concatenate([small_r[0], small_r[1]], 0)
     turned = mm_nt(eye, edges).astype(BF16)
     turned_s = mm_nt(eye, edges_s).astype(BF16)
     col_main = mm(turned, sel_a)
@@ -499,12 +564,16 @@
         before = jnp.where(is0, far[8:16], near[8:16])
         return jnp.concatenate([main, after, before], 0)
 
+    def twice(x):
+        rows = x.astype(F32)[8:16]
+        return jnp.concatenate([rows, rows], 0)
+
     col_far16 = jnp.concatenate([col_far[0:8], col_far[120:128]], 0)
     col_small16 = jnp.concatenate([col_small[0:8], col_small[120:128]], 0)
     received = add_part(
-        [msg_r[0, 32:160].astype(F32), msg_r[1, 32:160].astype(F32), col_main],
-        [msg_r[0, 16:32].astype(F32), msg_r[1, 16:32].astype(F32), col_far16],
-        [small_r[0, 16:32].astype(F32), small_r[1, 16:32].astype(F32), col_small16],
+        [msg_r[0, 16:EXT].astype(F32), msg_r[1, 16:EXT].astype(F32), col_main],
+        [twice(msg_r[0, 0:16]), twice(msg_r[1, 0:16]), col_far16],
+        [twice(small_r[0]), twice(small_r[1]), col_small16],
     )
     speed = SPEED_GAIN * (grad + received) * final[:, LANES : 2 * LANES]
 
@@ -538,9 +607,19 @@
     cp_resist.wait()
     cp_out.wait()
 
+    @pl.when(straight)
+    def _():
+        fl.wait_send()
+        fr.wait_send()
+
+    @pl.when(hops)
+    def _():
+        for d in (kl, kr_, ol, orr):
+            d.wait_send()
+
     @pl.when(send_ok)
     def _():
-        for d in (fl, fr, ml, mr, nl, nr):
+        for d in (ml, mr, nl, nr):
             d.wait_send()
 
     @pl.when(has_l)
@@ -615,14 +694,15 @@
                 pltpu.VMEM((3, KF, 2 * KF), BF16),
                 pltpu.VMEM((2 * KF, WIN), F32),
                 pltpu.VMEM((2 * KF, WIN), F32),
-                pltpu.VMEM((2, 160, 128), BF16),
-                pltpu.VMEM((2, 160, 128), BF16),
-                pltpu.VMEM((2, 32, 128), BF16),
-                pltpu.VMEM((2, 32, 128), BF16),
+                pltpu.VMEM((2, EXT, 128), BF16),
+                pltpu.VMEM((2, EXT, 128), BF16),
+                pltpu.VMEM((2, 16, 128), BF16),
+                pltpu.VMEM((2, 16, 128), BF16),
                 pltpu.VMEM((EXT, 2 * LANES), F32),
+                pltpu.VMEM((2, 128, 128), BF16),
                 dma((5,)),
                 dma((2,)),
-                dma((18,)),
+                dma((22,)),
                 dma((2,)),
                 dma((2,)),
                 dma((2, 2)),
@@ -632,11 +712,14 @@
                 dma((2,)),
                 dma((2,)),
                 dma,
+                dma((2,)),
+                pltpu.SemaphoreType.REGULAR,
+                pltpu.SemaphoreType.REGULAR,
             ],
             compiler_params=pltpu.CompilerParams(
                 collective_id=0,
                 has_side_effects=True,
-                vmem_limit_bytes=62 * 1024 * 1024,
+                vmem_limit_bytes=54600 * 1024,
             ),
             cost_estimate=pl.CostEstimate(
                 flops=1_500_000_000, bytes_accessed=6_000_000, transcendentals=400_000

time: 83 us -> 71.3 us (0.86)
  the two profiles are of different devices: /device:TPU:7 before, /device:TPU:165 now
where the time goes in v2:
time: 71.3 us; the launch traced here: 71.2 us
  Pallas kernels  68.5 us (96%)
  local copies, waits for them, and re-layouts  1.41 us (2%)
  between operations  1.29 us (2%)
    pallas_call x1, Pallas kernels, body(): pl.pallas_call(whole, out_shape=(jax.ShapeDtypeStruct((1, TILE, TILE), F3...  68.5 us

profile of v2, /device:TPU:165, one launch (start us, length us, event | category | flops | bytes accessed | tf_op | source)
XLA Modules:
  0.0 71.2 jit_solution(15815867748728563004)
XLA Ops:
  1.3 68.5 %shard_map.77 = (f32[1,256,256]{2,1,0:T(8,128)S(1)}, f32[256,256]{1,0:T(8,128)S(1)}) custom-call(s32[256,256]{1,0:T(8,128)} %args_0_.4, s32[256,256]{1,0:T(8,128)} %args_1_.4, f32[1,5,2,128,128]{4,3,2,1,0:T(8,128)} %args_2_.4, f32[1]{0:T(128)S(6)} %copy.10.args_3_, bf16[768,512]{1,0:T(8,128)(2,1)} %constant.4.clone.args_4_, ...), custom_call_target="tpu_custom_call" | custom-call | flops 1500000000 | bytes 6000000 | tf_op jit(solution)/shard_map/pallas_call | solution.py:664
  69.8 0.7 copy.11
  70.5 0.7 copy.12

commit v3 on v2

--- a/solution.py
+++ b/solution.py
@@ -107,6 +107,7 @@
     trw,
     spec,
     fields,
+    proj,
     inten,
     sens2,
     resist,
@@ -187,6 +188,24 @@
             device_id_type=MESH,
         ).wait_recv()
 
+    started = []
+
+    def start(cond, *copies):
+        started.append((cond, copies))
+
+        @pl.when(cond)
+        def _():
+            for d in copies:
+                d.start()
+
+    def settle():
+        for cond, copies in started:
+
+            @pl.when(cond)
+            def _(copies=copies):
+                for d in copies:
+                    d.wait_send()
+
     cp_level = local(level_hbm, level_i, in_sem.at[0])
     cp_a = local(a_hbm, ta, in_sem.at[1])
     cp_kern = local(kern_hbm, kern, in_sem.at[2])
@@ -266,28 +285,15 @@
     sl = remote(2, win.at[1, pl.ds(128, 256)], win.at[3, pl.ds(128, 256)], s_side.at[1], left)
     sr = remote(3, win.at[2, pl.ds(128, 256)], win.at[0, pl.ds(128, 256)], s_side.at[0], right)
 
-    kl = remote(18, win.at[1, pl.ds(srow, 128)], held.at[0], s_held.at[0], (a, bp, c))
-    kr_ = remote(19, win.at[2, pl.ds(srow, 128)], held.at[1], s_held.at[1], (a, bp, c))
-    ol = remote(20, held.at[0], win.at[jnp.where(bp > 0, 3, 1), pl.ds(hrow, 128)], s_far.at[1 - zpl], (far_row, bpl, c))
-    orr = remote(21, held.at[1], win.at[jnp.where(bp < n_tx - 1, 0, 2), pl.ds(hrow, 128)], s_far.at[zpr], (far_row, bpr, c))
-
-    @pl.when(straight)
-    def _():
-        fl.start()
-        fr.start()
-
-    @pl.when(hops)
-    def _():
-        kl.start()
-        kr_.start()
-
-    @pl.when(has_l)
-    def _():
-        sl.start()
-
-    @pl.when(has_r)
-    def _():
-        sr.start()
+    kl = remote(24, win.at[1, pl.ds(srow, 128)], held.at[0], s_held.at[0], (a, bp, c))
+    kr_ = remote(25, win.at[2, pl.ds(srow, 128)], held.at[1], s_held.at[1], (a, bp, c))
+    ol = remote(26, held.at[0], win.at[jnp.where(bp > 0, 3, 1), pl.ds(hrow, 128)], s_far.at[1 - zpl], (far_row, bpl, c))
+    orr = remote(27, held.at[1], win.at[jnp.where(bp < n_tx - 1, 0, 2), pl.ds(hrow, 128)], s_far.at[zpr], (far_row, bpr, c))
+
+    start(hops, kl, kr_)
+    start(straight, fl, fr)
+    start(has_l, sl)
+    start(has_r, sr)
 
     @pl.when(jnp.logical_not(has_l))
     def _():
@@ -347,114 +353,112 @@
         arrived(held.at[1], s_held.at[1])
         orr.start()
 
+    started.append((hops, (ol, orr)))
+
     blk_l, blk_r = jnp.where(has_l, 0, 1), jnp.where(has_r, 3, 2)
-    got_l, got_r = win.at[blk_l, pl.ds(hrow, 128)], win.at[blk_r, pl.ds(hrow, 128)]
-    pl_ = remote(4, got_l, got_l, s_part.at[0], partner)
-    pr_ = remote(5, got_r, got_r, s_part.at[1], partner)
-    fan_l = [remote(6 + d, got_l, win.at[2, pl.ds(hrow, 128)], s_fan.at[c, 1], (a, b - 1, d)) for d in (0, 1)]
-    fan_r = [remote(8 + d, got_r, win.at[1, pl.ds(hrow, 128)], s_fan.at[c, 0], (a, b + 1, d)) for d in (0, 1)]
-
-    @pl.when(recv_ok)
-    def _():
-        arrived(got_l, s_far.at[0])
-
-        @pl.when(has_l)
-        def _():
-            fan_l[0].start()
-            fan_l[1].start()
-
-        pl_.start()
-        arrived(got_r, s_far.at[1])
-
-        @pl.when(has_r)
-        def _():
-            fan_r[0].start()
-            fan_r[1].start()
-
-        pr_.start()
-
-    @pl.when(small_ok)
-    def _():
-        orow = pl.multiple_of(384 * other, 128)
-        arrived(win.at[blk_l, pl.ds(orow, 128)], s_part.at[0])
-        arrived(win.at[blk_r, pl.ds(orow, 128)], s_part.at[1])
-
-    for d, ok in ((0, up_ok), (1, dn_ok)):
+    first = jnp.where(late_up | early_up, 1, jnp.where(late_dn | early_dn, 0, c))
+    for step in range(2):
+        d = first if step == 0 else 1 - first
+        ok = jnp.where(d == 0, up_ok.astype(jnp.int32), dn_ok.astype(jnp.int32)) > 0
+        mine, theirs = ok & (d == c), ok & (d != c)
+        hr_ = pl.multiple_of(384 * d, 128)
+        got_l, got_r = win.at[blk_l, pl.ds(hr_, 128)], win.at[blk_r, pl.ds(hr_, 128)]
+        n0 = 4 + 6 * step
+        part_l = remote(n0, got_l, got_l, s_part.at[0], partner)
+        part_r = remote(n0 + 1, got_r, got_r, s_part.at[1], partner)
+        fan_l = [
+            remote(n0 + 2 + e, got_l, win.at[2, pl.ds(hr_, 128)], s_fan.at[d, 1], (a, b - 1, e))
+            for e in (0, 1)
+        ]
+        fan_r = [
+            remote(n0 + 4 + e, got_r, win.at[1, pl.ds(hr_, 128)], s_fan.at[d, 0], (a, b + 1, e))
+            for e in (0, 1)
+        ]
+
+        @pl.when(mine)
+        def _(got=got_l):
+            arrived(got, s_far.at[0])
+
+        start(mine & has_l, *fan_l)
+        start(mine, part_l)
+
+        @pl.when(mine)
+        def _(got=got_r):
+            arrived(got, s_far.at[1])
+
+        start(mine & has_r, *fan_r)
+        start(mine, part_r)
+
+        @pl.when(theirs)
+        def _(got_l=got_l, got_r=got_r):
+            arrived(got_l, s_part.at[0])
+            arrived(got_r, s_part.at[1])
+
         @pl.when(ok & has_l)
-        def _(d=d):
-            arrived(win.at[1, pl.ds(384 * d, 128)], s_fan.at[d, 0])
+        def _(hr_=hr_, d=d):
+            arrived(win.at[1, pl.ds(hr_, 128)], s_fan.at[d, 0])
 
         @pl.when(ok & has_r)
-        def _(d=d):
-            arrived(win.at[2, pl.ds(384 * d, 128)], s_fan.at[d, 1])
-
-    for blk in range(4):
-        to_trans(blk, 0, 128)
-        to_trans(blk, 384, 128)
-    lift_b = (
-        lift[...]
-        + mm(ta[A_FWD : A_FWD + 256, 0:128], trw[0:128, :])
-        + mm(ta[A_FWD : A_FWD + 256, 384:512], trw[384:512, :])
-    ).astype(BF16)
+        def _(hr_=hr_, d=d):
+            arrived(win.at[2, pl.ds(hr_, 128)], s_fan.at[d, 1])
+
+        x = jnp.concatenate([win[blk, pl.ds(hr_, 128)] for blk in range(4)], 1)
+        x = jnp.tanh(0.25 * x.astype(F32)).astype(BF16)
+        lift[...] += mm(ta[A_FWD : A_FWD + 256, pl.ds(hr_, 128)], x)
+    lift_b = lift[...].astype(BF16)
     s = mm(lift_b, tb[B_FT : B_FT + 512])
     spec[0] = s[:128, :128] - s[128:, 128:]
     spec[1] = s[:128, 128:] + s[128:, :128]
 
     dose = dose_ref[0]
-    inten[...] = jnp.zeros_like(inten)
-
-    def ahead(k, _):
+    sre, sim = spec[0], spec[1]
+    for k in range(KERNELS):
         kr, ki = kern[0, k, 0], kern[0, k, 1]
-        sre, sim = spec[0], spec[1]
         bre = (kr * sre - ki * sim).astype(BF16)
         bim = (kr * sim + ki * sre).astype(BF16)
         blur = jnp.concatenate(
             [jnp.concatenate([bre, bim], 1), jnp.concatenate([-bim, bre], 1)], 0
         )
-        proj = mm(tb[B_INV : B_INV + 256], blur).astype(BF16)
-        field = mm(proj, ta[A_FIELD : A_FIELD + 256])
-        fields[k] = field
-        fre, fim = field[:, :256], field[:, 256:]
-        inten[...] += fre * fre + fim * fim
-        return 0
-
-    lax.fori_loop(0, KERNELS, ahead, 0)
+        proj[256 * k : 256 * k + 256] = mm(tb[B_INV : B_INV + 256], blur).astype(BF16)
+    for k in range(KERNELS):
+        fields[k] = mm(proj[256 * k : 256 * k + 256], ta[A_FIELD : A_FIELD + 256])
+    total = jnp.zeros((TILE, TILE), F32)
+    for k in range(KERNELS):
+        fre, fim = fields[k, :, :256], fields[k, :, 256:]
+        total = total + (fre * fre + fim * fim)
+    inten[...] = total
 
     res = jax.nn.sigmoid(STEEPNESS * (dose * inten[...] - THRESHOLD))
     resist[...] = res
     cp_resist = local(resist, resist_hbm.at[0], out_sem.at[0])
     goal = target_i[...].astype(F32)
     sens2[...] = 2.0 * (2.0 * (res - goal) * STEEPNESS * dose * res * (1.0 - res))
-    gacc[...] = jnp.zeros_like(gacc)
-
-    def back(k, _):
+    s2 = jnp.concatenate([sens2[...], sens2[...]], 1)
+    for k in range(KERNELS):
+        adj = (s2 * fields[k]).astype(BF16)
+        proj[256 * k : 256 * k + 256] = mm(adj, tb[B_BACK : B_BACK + 512]).astype(BF16)
+    acc_re = jnp.zeros((KF, KF), F32)
+    acc_im = jnp.zeros((KF, KF), F32)
+    for k in range(KERNELS):
         kr, ki = kern[0, k, 0], kern[0, k, 1]
-        s2 = sens2[...]
-        adj = (jnp.concatenate([s2, s2], 1) * fields[k]).astype(BF16)
-        bk = mm(adj, tb[B_BACK : B_BACK + 512]).astype(BF16)
-        g = mm(tb[B_INVT : B_INVT + 256], bk)
+        g = mm(tb[B_INVT : B_INVT + 256], proj[256 * k : 256 * k + 256])
         gre = g[:128, :128] + g[128:, 128:]
         gim = g[:128, 128:] - g[128:, :128]
-        gacc[:, :128] += kr * gre + ki * gim
-        gacc[:, 128:] += kr * gim - ki * gre
-        return 0
-
-    lax.fori_loop(0, KERNELS, back, 0)
-
-    cc = remote(10, gacc, gother, s_corner, partner)
+        acc_re = acc_re + (kr * gre + ki * gim)
+        acc_im = acc_im + (kr * gim - ki * gre)
+    gacc[:, :128] = acc_re
+    gacc[:, 128:] = acc_im
+
+    cc = remote(16, gacc, gother, s_corner, partner)
     cc.start()
+    started.append((c >= 0, (cc,)))
     arrived(gother, s_corner)
     hbuf[1] = (gacc[...] + gother[...]).astype(BF16)
-    hl = remote(11, hbuf.at[1], hbuf.at[2], s_spec.at[1], left)
-    hr = remote(12, hbuf.at[1], hbuf.at[0], s_spec.at[0], right)
-
-    @pl.when(has_l)
-    def _():
-        hl.start()
-
-    @pl.when(has_r)
-    def _():
-        hr.start()
+    hl = remote(17, hbuf.at[1], hbuf.at[2], s_spec.at[1], left)
+    hr = remote(18, hbuf.at[1], hbuf.at[0], s_spec.at[0], right)
+
+    start(has_l, hl)
+    start(has_r, hr)
 
     glift[0:128] = mm(hbuf[1], ta[A_FWD : A_FWD + 256])
     glift[128:256] = mm(hbuf[1], ta[A_TURN : A_TURN + 256])
@@ -511,21 +515,16 @@
         tail_rows = jnp.where(is0, part[136:144], part[16:24])
         small_s[side] = jnp.concatenate([edge, tail_rows], 0).astype(BF16)
 
-    ml = remote(13, msg_s.at[0], msg_r.at[1 - zl], s_msg.at[1 - zl], (ar, bl, c))
-    mr = remote(14, msg_s.at[1], msg_r.at[zr], s_msg.at[zr], (ar, br, c))
-    nl = remote(15, small_s.at[0], small_r.at[1 - zl], s_small.at[1 - zl], (ar, bl, other))
-    nr = remote(16, small_s.at[1], small_r.at[zr], s_small.at[zr], (ar, br, other))
+    ml = remote(19, msg_s.at[0], msg_r.at[1 - zl], s_msg.at[1 - zl], (ar, bl, c))
+    mr = remote(20, msg_s.at[1], msg_r.at[zr], s_msg.at[zr], (ar, br, c))
+    nl = remote(21, small_s.at[0], small_r.at[1 - zl], s_small.at[1 - zl], (ar, bl, other))
+    nr = remote(22, small_s.at[1], small_r.at[zr], s_small.at[zr], (ar, br, other))
 
     @pl.when(hops)
     def _():
         pl.semaphore_wait(ready, 4)
 
-    @pl.when(send_ok)
-    def _():
-        ml.start()
-        mr.start()
-        nl.start()
-        nr.start()
+    start(send_ok, ml, mr, nl, nr)
 
     ring_lane = lax.broadcasted_iota(jnp.int32, (256, 128), 1)
     gl_ring = jnp.where(ring_lane < 64, gblk[3], gblk[0]).astype(BF16)
@@ -600,55 +599,14 @@
 
     mine = out_hbm.at[pl.ds(pl.multiple_of(128 * c, 128), 128)]
     result = final.at[pl.ds(0, 128), pl.ds(0, 256)]
-    ff = remote(17, result, mine, s_final, partner)
+    ff = remote(23, result, mine, s_final, partner)
     ff.start()
+    started.append((c >= 0, (ff,)))
     cp_out = local(result, mine, out_sem.at[1])
 
     cp_resist.wait()
     cp_out.wait()
-
-    @pl.when(straight)
-    def _():
-        fl.wait_send()
-        fr.wait_send()
-
-    @pl.when(hops)
-    def _():
-        for d in (kl, kr_, ol, orr):
-            d.wait_send()
-
-    @pl.when(send_ok)
-    def _():
-        for d in (ml, mr, nl, nr):
-            d.wait_send()
-
-    @pl.when(has_l)
-    def _():
-        sl.wait_send()
-        hl.wait_send()
-
-    @pl.when(has_r)
-    def _():
-        sr.wait_send()
-        hr.wait_send()
-
-    @pl.when(recv_ok)
-    def _():
-        pl_.wait_send()
-        pr_.wait_send()
-
-    @pl.when(recv_ok & has_l)
-    def _():
-        fan_l[0].wait_send()
-        fan_l[1].wait_send()
-
-    @pl.when(recv_ok & has_r)
-    def _():
-        fan_r[0].wait_send()
-        fan_r[1].wait_send()
-
-    cc.wait_send()
-    ff.wait_send()
+    settle()
     arrived(out_hbm.at[pl.ds(pl.multiple_of(128 * other, 128), 128)], s_final)
 
 
@@ -686,6 +644,7 @@
                 pltpu.VMEM((WIN, WIN), BF16),
                 pltpu.VMEM((2, KF, KF), F32),
                 pltpu.VMEM((KERNELS, TILE, 2 * TILE), F32),
+                pltpu.VMEM((KERNELS * TILE, TILE), BF16),
                 pltpu.VMEM((TILE, TILE), F32),
                 pltpu.VMEM((TILE, TILE), F32),
                 pltpu.VMEM((TILE, TILE), F32),
@@ -702,7 +661,7 @@
                 pltpu.VMEM((2, 128, 128), BF16),
                 dma((5,)),
                 dma((2,)),
-                dma((22,)),
+                dma((28,)),
                 dma((2,)),
                 dma((2,)),
                 dma((2, 2)),

time: 71.3 us -> 68.6 us (0.962)
  the two profiles are of different devices: /device:TPU:165 before, /device:TPU:189 now
where the time goes in v3:
time: 68.6 us; the launch traced here: 68.5 us
  Pallas kernels  65.8 us (96%)
  local copies, waits for them, and re-layouts  1.41 us (2%)
  between operations  1.29 us (2%)
    pallas_call x1, Pallas kernels, body(): pl.pallas_call(whole, out_shape=(jax.ShapeDtypeStruct((1, TILE, TILE), F3...  65.8 us
    unnamed x2, local copies, waits for them, and re-layouts  1.41 us

profile of v3, /device:TPU:189, one launch (start us, length us, event | category | flops | bytes accessed | tf_op | source)
XLA Modules:
  0.0 68.5 jit_solution(17009635079268731673)
XLA Ops:
  1.3 65.8 %shard_map.77 = (f32[1,256,256]{2,1,0:T(8,128)S(1)}, f32[256,256]{1,0:T(8,128)S(1)}) custom-call(s32[256,256]{1,0:T(8,128)} %args_0_.4, s32[256,256]{1,0:T(8,128)} %args_1_.4, f32[1,5,2,128,128]{4,3,2,1,0:T(8,128)} %args_2_.4, f32[1]{0:T(128)S(6)} %copy.10.args_3_, bf16[768,512]{1,0:T(8,128)(2,1)} %constant.4.clone.args_4_, ...), custom_call_target="tpu_custom_call" | custom-call | flops 1500000000 | bytes 6000000 | tf_op jit(solution)/shard_map/pallas_call | solution.py:622
  67.1 0.7 %copy.11 = f32[1,256,256]{2,1,0:T(8,128)} copy(f32[1,256,256]{2,1,0:T(8,128)S(1)} %get-tuple-element.4) | data formatting | bytes 524288
  67.8 0.7 %copy.12 = f32[256,256]{1,0:T(8,128)} copy(f32[256,256]{1,0:T(8,128)S(1)} %get-tuple-element.5) | data formatting | bytes 524288

commit v4 on v3

--- a/solution.py
+++ b/solution.py
@@ -121,6 +121,7 @@
     small_s,
     small_r,
     final,
+    done,
     held,
     in_sem,
     out_sem,
@@ -206,46 +207,46 @@
                 for d in copies:
                     d.wait_send()
 
+    barrier = pltpu.get_barrier_semaphore()
+
+    def hello(dev):
+        pl.semaphore_signal(barrier, inc=1, device_id=dev, device_id_type=MESH)
+
+    @pl.when(hops)
+    def _():
+        hello((a, bp, c))
+        hello((far_row, bl, c))
+        hello((far_row, br, c))
+        hello((far_row, bpl, c))
+        hello((far_row, bpr, c))
+
+    @pl.when(up_ok & jnp.logical_not(late_up))
+    def _():
+        hello((a - 1, bl, 0))
+        hello((a - 1, br, 0))
+
+    @pl.when(dn_ok & jnp.logical_not(late_dn))
+    def _():
+        hello((a + 1, bl, 1))
+        hello((a + 1, br, 1))
+
+    hello(partner)
+
+    @pl.when(has_l)
+    def _():
+        hello((a, b - 1, 0))
+        hello((a, b - 1, 1))
+
+    @pl.when(has_r)
+    def _():
+        hello((a, b + 1, 0))
+        hello((a, b + 1, 1))
+
     cp_level = local(level_hbm, level_i, in_sem.at[0])
     cp_a = local(a_hbm, ta, in_sem.at[1])
     cp_kern = local(kern_hbm, kern, in_sem.at[2])
     cp_b = local(b_hbm, tb, in_sem.at[3])
     cp_target = local(target_hbm, target_i, in_sem.at[4])
-
-    barrier = pltpu.get_barrier_semaphore()
-
-    def hello(dev):
-        pl.semaphore_signal(barrier, inc=1, device_id=dev, device_id_type=MESH)
-
-    @pl.when(up_ok & jnp.logical_not(late_up))
-    def _():
-        hello((a - 1, bl, 0))
-        hello((a - 1, br, 0))
-
-    @pl.when(dn_ok & jnp.logical_not(late_dn))
-    def _():
-        hello((a + 1, bl, 1))
-        hello((a + 1, br, 1))
-
-    @pl.when(hops)
-    def _():
-        hello((a, bp, c))
-        hello((far_row, bl, c))
-        hello((far_row, br, c))
-        hello((far_row, bpl, c))
-        hello((far_row, bpr, c))
-
-    hello(partner)
-
-    @pl.when(has_l)
-    def _():
-        hello((a, b - 1, 0))
-        hello((a, b - 1, 1))
-
-    @pl.when(has_r)
-    def _():
-        hello((a, b + 1, 0))
-        hello((a, b + 1, 1))
 
     cp_level.wait()
     level0 = level_i[...].astype(F32) * 0.125
@@ -263,11 +264,6 @@
     )
     pl.semaphore_wait(barrier, wanted)
 
-    @pl.when(late)
-    def _():
-        for to in (bl, br):
-            pl.semaphore_signal(ready, inc=1, device_id=(far_row, to, far_core), device_id_type=MESH)
-
     @pl.when(meets)
     def _():
         for to in (bl, br):
@@ -277,6 +273,11 @@
                 device_id=(far_row, (to + half) % n_tx, far_core),
                 device_id_type=MESH,
             )
+
+    @pl.when(late)
+    def _():
+        for to in (bl, br):
+            pl.semaphore_signal(ready, inc=1, device_id=(far_row, to, far_core), device_id_type=MESH)
 
     srow = pl.multiple_of(256 - 128 * c, 128)
     hrow = pl.multiple_of(384 * c, 128)
@@ -595,10 +596,10 @@
         spread = up + down + lf + rt - 4.0 * level
         level = level - speed * jnp.sqrt(GRAD_FLOOR + sy * sy + sx * sx) + SMOOTHING * spread
         level = jnp.where(inside, level, 0.0)
-    final[0:128, 0:256] = level[0:128, 0:256]
+    done[...] = level[0:128, 0:256]
 
     mine = out_hbm.at[pl.ds(pl.multiple_of(128 * c, 128), 128)]
-    result = final.at[pl.ds(0, 128), pl.ds(0, 256)]
+    result = done
     ff = remote(23, result, mine, s_final, partner)
     ff.start()
     started.append((c >= 0, (ff,)))
@@ -658,6 +659,7 @@
                 pltpu.VMEM((2, 16, 128), BF16),
                 pltpu.VMEM((2, 16, 128), BF16),
                 pltpu.VMEM((EXT, 2 * LANES), F32),
+                pltpu.VMEM((128, TILE), F32),
                 pltpu.VMEM((2, 128, 128), BF16),
                 dma((5,)),
                 dma((2,)),

time: 68.6 us -> 68.4 us (level)
  no operation moved by 1% of the time
where the time goes in v4:
time: 68.4 us; the launch traced here: 68.3 us
  Pallas kernels  65.6 us (96%)
  local copies, waits for them, and re-layouts  1.41 us (2%)
  between operations  1.29 us (2%)
    pallas_call x1, Pallas kernels, body(): pl.pallas_call(whole, out_shape=(jax.ShapeDtypeStruct((1, TILE, TILE), F3...  65.6 us
    unnamed x2, local copies, waits for them, and re-layouts  1.41 us

profile of v4, /device:TPU:189, one launch (start us, length us, event | category | flops | bytes accessed | tf_op | source)
XLA Modules:
  0.0 68.3 jit_solution(2795256473786484250)
XLA Ops:
  1.3 65.6 %shard_map.77 = (f32[1,256,256]{2,1,0:T(8,128)S(1)}, f32[256,256]{1,0:T(8,128)S(1)}) custom-call(s32[256,256]{1,0:T(8,128)} %args_0_.4, s32[256,256]{1,0:T(8,128)} %args_1_.4, f32[1,5,2,128,128]{4,3,2,1,0:T(8,128)} %args_2_.4, f32[1]{0:T(128)S(6)} %copy.10.args_3_, bf16[768,512]{1,0:T(8,128)(2,1)} %constant.4.clone.args_4_, ...), custom_call_target="tpu_custom_call" | custom-call | flops 1500000000 | bytes 6000000 | tf_op jit(solution)/shard_map/pallas_call | solution.py:623
  66.9 0.7 %copy.11 = f32[1,256,256]{2,1,0:T(8,128)} copy(f32[1,256,256]{2,1,0:T(8,128)S(1)} %get-tuple-element.4) | data formatting | bytes 524288
  67.6 0.7 %copy.12 = f32[256,256]{1,0:T(8,128)} copy(f32[256,256]{1,0:T(8,128)S(1)} %get-tuple-element.5) | data formatting | bytes 524288

commit v5 on v3

--- a/solution.py
+++ b/solution.py
@@ -504,6 +504,15 @@
     picked = jnp.concatenate([mm_nt(pick_l, gl[:, 128:256]), mm_nt(pick_r, gl[:, 256:384])], 0)
     crossed = mm(picked.astype(BF16), tb[pl.ds(pl.multiple_of(B_CROSS + 256 * c, 16), 256)])
     row16 = lax.broadcasted_iota(jnp.int32, (16, 128), 0)
+    ml = remote(19, msg_s.at[0], msg_r.at[1 - zl], s_msg.at[1 - zl], (ar, bl, c))
+    mr = remote(20, msg_s.at[1], msg_r.at[zr], s_msg.at[zr], (ar, br, c))
+    nl = remote(21, small_s.at[0], small_r.at[1 - zl], s_small.at[1 - zl], (ar, bl, other))
+    nr = remote(22, small_s.at[1], small_r.at[zr], s_small.at[zr], (ar, br, other))
+
+    @pl.when(hops)
+    def _():
+        pl.semaphore_wait(ready, 4)
+
     for side in range(2):
         cols = slice(128 * side, 128 * side + 128)
         cr = crossed[16 * side : 16 * side + 16]
@@ -514,17 +523,8 @@
         msg_s[side, 16:EXT] = part[16:EXT].astype(BF16)
         tail_rows = jnp.where(is0, part[136:144], part[16:24])
         small_s[side] = jnp.concatenate([edge, tail_rows], 0).astype(BF16)
-
-    ml = remote(19, msg_s.at[0], msg_r.at[1 - zl], s_msg.at[1 - zl], (ar, bl, c))
-    mr = remote(20, msg_s.at[1], msg_r.at[zr], s_msg.at[zr], (ar, br, c))
-    nl = remote(21, small_s.at[0], small_r.at[1 - zl], s_small.at[1 - zl], (ar, bl, other))
-    nr = remote(22, small_s.at[1], small_r.at[zr], s_small.at[zr], (ar, br, other))
-
-    @pl.when(hops)
-    def _():
-        pl.semaphore_wait(ready, 4)
-
-    start(send_ok, ml, mr, nl, nr)
+        start(send_ok, *((ml, nl), (mr, nr))[side])
+
 
     ring_lane = lax.broadcasted_iota(jnp.int32, (256, 128), 1)
     gl_ring = jnp.where(ring_lane < 64, gblk[3], gblk[0]).astype(BF16)

time: 68.6 us -> 68.6 us (level)
  no operation moved by 1% of the time
where the time goes in v5:
time: 68.6 us; the launch traced here: 68.5 us
  Pallas kernels  65.8 us (96%)
  local copies, waits for them, and re-layouts  1.41 us (2%)
  between operations  1.29 us (2%)
    pallas_call x1, Pallas kernels, body(): pl.pallas_call(whole, out_shape=(jax.ShapeDtypeStruct((1, TILE, TILE), F3...  65.8 us
    unnamed x2, local copies, waits for them, and re-layouts  1.41 us

profile of v5, /device:TPU:189, one launch (start us, length us, event | category | flops | bytes accessed | tf_op | source)
XLA Modules:
  0.0 68.5 jit_solution(17306238793337901038)
XLA Ops:
  1.3 65.8 %shard_map.77 = (f32[1,256,256]{2,1,0:T(8,128)S(1)}, f32[256,256]{1,0:T(8,128)S(1)}) custom-call(s32[256,256]{1,0:T(8,128)} %args_0_.4, s32[256,256]{1,0:T(8,128)} %args_1_.4, f32[1,5,2,128,128]{4,3,2,1,0:T(8,128)} %args_2_.4, f32[1]{0:T(128)S(6)} %copy.10.args_3_, bf16[768,512]{1,0:T(8,128)(2,1)} %constant.4.clone.args_4_, ...), custom_call_target="tpu_custom_call" | custom-call | flops 1500000000 | bytes 6000000 | tf_op jit(solution)/shard_map/pallas_call | solution.py:622
  67.1 0.7 %copy.11 = f32[1,256,256]{2,1,0:T(8,128)} copy(f32[1,256,256]{2,1,0:T(8,128)S(1)} %get-tuple-element.4) | data formatting | bytes 524288
  67.8 0.7 %copy.12 = f32[256,256]{1,0:T(8,128)} copy(f32[256,256]{1,0:T(8,128)S(1)} %get-tuple-element.5) | data formatting | bytes 524288
